TPU v7x, 512 devices: a whole 4x4x16 slice. The times are simulated.
512 devices in a mesh: dp: 4 (over x), ctx: 32 (over y, z_lo), tensor: 4 (over z_hi, core).
Axes of the slice: x: 4, y: 4, z: 16 (z_hi: 2, z_lo: 8; z = z_hi * 8 + z_lo), core: 2. Of those that a mesh axis runs over, the one named last changes fastest.
Arguments:
- queries: bfloat16 [4, 4096, 2048], P('dp', 'ctx', 'tensor'), may hold values from -64 to 64
- neighbours: bfloat16 [4, 64, 256, 896], P('dp', 'ctx'), may hold values from -64 to 64
- key_weight: bfloat16 [896, 2048], P(None, 'tensor'), may hold values from -1 to 1
- value_weight: bfloat16 [896, 2048], P(None, 'tensor'), may hold values from -0.1875 to 0.1875
- neighbour_ids: int32 [4, 64, 256], P('dp', 'ctx'), may hold values from 0 to 127999, as said below
- block_document: int32 [4, 64], P('dp', 'ctx'), may hold values from 0 to 7, never falling along the last dimension, each value on 1 to 16 neighbouring positions
- grad_out: bfloat16 [4, 4096, 2048], P('dp', 'ctx', 'tensor'), may hold values from -6 to 6
Outputs:
- attended: bfloat16 [4, 4096, 2048], P('dp', 'ctx', 'tensor')
- grad_queries: bfloat16 [4, 4096, 2048], P('dp', 'ctx', 'tensor')
- grad_neighbours: bfloat16 [4, 64, 256, 896], P('dp', 'ctx')
- grad_key_weight: float32 [896, 2048], P(('dp', 'ctx'), 'tensor')
- grad_value_weight: float32 [896, 2048], P(('dp', 'ctx'), 'tensor')
Inputs may be any that keep to these rules, and one draw needn't show every extreme that they name: `neighbour_ids`: id 0 marks a padding token; in each of the 2 neighbours of 128 tokens the padding tokens follow all real ones, and the first quarter of the 128 tokens is real. `block_document`: the document numbers of a sequence's stretches never fall.
All inputs are finite; a program needn't handle non-finite values.
Results may differ from a plain program's by a relative error of at most 0.015.
The roundings to bfloat16 on the way count: a program that leaves them out, or rounds other values in their place, can miss the bound.
Values may be sent and summed in bfloat16 or wider, within the bound.
No kernel may reach another device: no remote copies, remote signals or barrier semaphores. Data moves between devices by JAX's collectives and lax.ppermute only.
A program may use at most 64 MiB of HBM per device.

v0:
```python
import jax
import jax.numpy as jnp
from jax import lax
from jax.sharding import PartitionSpec as P

HEAD_DIM = 128
STRETCH = 64


masked_score = -1e30


def from_behind(block, axis, distance):
    devices = range(lax.axis_size(axis))
    route = [(i - distance, i) for i in devices if i - distance in devices]
    return lax.ppermute(block, axis, route)


def block_attention(query_blocks, source_keys, source_values, source_ids, block_gate, grad_blocks):
    score_scale = HEAD_DIM ** (-0.5)
    scores = (
        jnp.einsum("cthd,cjhd->chtj", query_blocks, source_keys, preferred_element_type=jnp.float32)
        * score_scale
    )
    usable = (source_ids != 0)[:, None, None, :]
    scores = jnp.where(usable, scores, masked_score)
    row_max = jnp.max(scores, axis=-1, keepdims=True)
    raised = jnp.exp(scores - row_max)
    weights = raised / jnp.sum(raised, axis=-1, keepdims=True)
    weights_half = weights.astype(jnp.bfloat16)
    gate_rows = block_gate[:, None, None, None]
    mixed = (
        jnp.einsum(
            "chtj,cjhd->cthd", weights_half, source_values, preferred_element_type=jnp.float32
        )
        * gate_rows
    )
    attended = mixed.astype(jnp.bfloat16)
    gated_grad = jnp.where(gate_rows > 0, grad_blocks, jnp.zeros_like(grad_blocks))
    grad_weights = jnp.einsum(
        "cthd,cjhd->chtj", gated_grad, source_values, preferred_element_type=jnp.float32
    )
    inner = jnp.sum(weights * grad_weights, axis=-1, keepdims=True)
    grad_scores = (weights * (grad_weights - inner) * score_scale).astype(jnp.bfloat16)
    grad_queries = jnp.einsum(
        "chtj,cjhd->cthd", grad_scores, source_keys, preferred_element_type=jnp.float32
    ).astype(jnp.bfloat16)
    grad_keys = jnp.einsum(
        "chtj,cthd->cjhd", grad_scores, query_blocks, preferred_element_type=jnp.float32
    ).astype(jnp.bfloat16)
    grad_values = jnp.einsum(
        "chtj,cthd->cjhd", weights_half, gated_grad, preferred_element_type=jnp.float32
    ).astype(jnp.bfloat16)
    return (attended, grad_queries, grad_keys, grad_values)


def project_rows(encodings, key_weight, value_weight):
    block_count = encodings.shape[0]
    slot_count = encodings.shape[1]
    flat_rows = encodings.reshape(block_count * slot_count, encodings.shape[2])
    head_count = key_weight.shape[1] // HEAD_DIM
    keys_part = jnp.dot(flat_rows, key_weight, preferred_element_type=jnp.float32).astype(
        jnp.bfloat16
    )
    values_part = jnp.dot(flat_rows, value_weight, preferred_element_type=jnp.float32).astype(
        jnp.bfloat16
    )
    return (
        keys_part.reshape(block_count, slot_count, head_count, HEAD_DIM),
        values_part.reshape(block_count, slot_count, head_count, HEAD_DIM),
    )


def head_partial(grad_keys, grad_values, key_weight, value_weight):
    block_count = grad_keys.shape[0]
    slot_count = grad_keys.shape[1]
    feature_width = key_weight.shape[1]
    flat_keys = grad_keys.reshape(block_count * slot_count, feature_width)
    flat_values = grad_values.reshape(block_count * slot_count, feature_width)
    contracted = (((1,), (1,)), ((), ()))
    partial_sum = lax.dot_general(
        flat_keys, key_weight, contracted, preferred_element_type=jnp.float32
    )
    partial_sum = partial_sum + lax.dot_general(
        flat_values, value_weight, contracted, preferred_element_type=jnp.float32
    )
    return partial_sum.reshape(block_count, slot_count, key_weight.shape[0])


def shards(queries, neighbours, key_weight, value_weight, neighbour_ids, block_document, grad_out):
    local_tokens = queries.shape[1]
    feature_width = queries.shape[2]
    block_total = neighbours.shape[1]
    slot_count = neighbours.shape[2]
    enc_width = neighbours.shape[3]
    head_count = feature_width // HEAD_DIM
    encodings = neighbours[0]
    token_ids = neighbour_ids[0]
    documents = block_document[0]
    prior_rows, prior_ids, prior_document = from_behind(
        (encodings[-1:], token_ids[-1:], documents[-1:]), "ctx", 1
    )
    source_rows = jnp.concatenate([prior_rows, encodings[:-1]], axis=0)
    source_keys, source_values = project_rows(source_rows, key_weight, value_weight)
    source_ids = jnp.concatenate([prior_ids, token_ids[:-1]], axis=0)
    previous = jnp.concatenate([prior_document, documents[:-1]], axis=0)
    global_block = lax.axis_index("ctx") * block_total + jnp.arange(block_total, dtype=jnp.int32)
    block_gate = jnp.logical_and(documents == previous, global_block >= 1).astype(jnp.float32)
    query_blocks = queries[0].reshape(block_total, STRETCH, head_count, HEAD_DIM)
    grad_blocks = grad_out[0].reshape(block_total, STRETCH, head_count, HEAD_DIM)
    attended, grad_queries, grad_keys, grad_values = block_attention(
        query_blocks, source_keys, source_values, source_ids, block_gate, grad_blocks
    )
    source_partial = head_partial(grad_keys, grad_values, key_weight, value_weight)
    back_partial = from_behind(source_partial[:1], "ctx", -1)
    partial_sum = jnp.concatenate([source_partial[1:], back_partial], axis=0)
    grad_rows = lax.psum(partial_sum, "tensor").astype(jnp.bfloat16)
    left_rows = source_rows.reshape(block_total * slot_count, enc_width)
    right_cols = jnp.concatenate(
        [
            grad_keys.reshape(block_total * slot_count, feature_width),
            grad_values.reshape(block_total * slot_count, feature_width),
        ],
        axis=1,
    )
    contracted = (((0,), (0,)), ((), ()))
    weight_grads = lax.psum_scatter(
        lax.dot_general(left_rows, right_cols, contracted, preferred_element_type=jnp.float32),
        ("dp", "ctx"),
        scatter_dimension=0,
        tiled=True,
    )
    return (
        attended.reshape(1, local_tokens, feature_width),
        grad_queries.reshape(1, local_tokens, feature_width),
        grad_rows[None],
        weight_grads[:, :feature_width],
        weight_grads[:, feature_width:],
    )


def solution(mesh):
    in_specs = (
        P("dp", "ctx", "tensor"),
        P("dp", "ctx", None, None),
        P(None, "tensor"),
        P(None, "tensor"),
        P("dp", "ctx", None),
        P("dp", "ctx"),
        P("dp", "ctx", "tensor"),
    )
    out_specs = (
        P("dp", "ctx", "tensor"),
        P("dp", "ctx", "tensor"),
        P("dp", "ctx", None, None),
        P(("dp", "ctx"), "tensor"),
        P(("dp", "ctx"), "tensor"),
    )
    return jax.shard_map(shards, mesh=mesh, in_specs=in_specs, out_specs=out_specs, check_vma=False)
```

profile of v0, /device:TPU:0, one launch (start us, length us, event | category | flops | bytes accessed | tf_op | source)
XLA Modules:
  0.0 2071.7 jit_solution(12649510752947424207)
XLA Ops:
  7.2 0.0 copy-start
  7.2 0.0 copy-start.5
  7.2 0.0 all-reduce.4.cloned.1.call-start
  7.3 1.4 slice_bitcast_fusion.3
  8.6 1.3 collective-permute-start
  10.0 0.6 fusion.54
  10.6 1.8 collective-permute-start.2
  12.4 3.0 collective-permute-start.1
  15.4 1.6 reshape_squeeze.7
  17.0 0.0 collective-permute-done.2
  17.0 1.3 broadcast_compare_fusion
  18.3 0.0 collective-permute-done.1
  18.4 0.0 copy-start.8
  18.4 0.8 copy-done.8
  19.1 1.1 pad_maximum_fusion.1
  20.3 1.5 convolution_convert_fusion.3
  21.8 1.2 reshape.107
  23.0 0.7 convolution_convert_fusion.2
  23.7 0.1 reshape.108
  23.8 0.0 copy-start.7
  23.8 0.3 convolution_multiply_fusion
  24.1 1.0 fusion.55
  25.2 1.1 fusion.23
  26.3 2.9 fusion.5
  29.2 4.8 fusion.4
  34.0 0.4 copy.39
  34.4 1.3 copy.40
  35.7 0.1 copy_bitcast_fusion
  35.9 3.0 fusion.13
  38.9 0.0 all-reduce.4.cloned.1.call-update
  38.9 0.0 copy-start.6
  38.9 0.7 fusion.44
  39.6 0.4 copy-done.6
  40.1 0.7 convolution_add_fusion
  40.8 1.0 slice_bitcast_fusion.1
  41.9 1.4 collective-permute-start.3
  43.3 1.3 dynamic-slice
  45.2 1.0 fusion.12
  46.2 0.1 copy.33
  46.3 0.7 reshape.109
  47.0 4.2 fusion.11
  51.2 0.1 copy.37
  51.3 0.7 reshape.110
  52.0 14.6 collective-permute-done.3
  66.6 1.6 pad_maximum_fusion
  68.2 116.5 %all-reduce.5 = bf16[2,256,896]{2,1,0:T(8,128)(2,1)} all-reduce(f32[2,256,896]{2,1,0:T(8,128)S(1)} %pad_maximum_fusion), channel_id=1, replica_groups=mesh['dp'=4,'ctx'=32,'tensor'=4] {'tensor'}, use_global_device_ids=true, to_apply=%region_3.4 | all-reduce | flops 458752 | bytes 2752512 | tf_op jit(solution)/shard_map/psum | solution.py:117
  184.7 1878.7 %all-reduce.4.cloned.1.call-done = f32[896,1024]{1,0:T(8,128)} async-done(((f32[896,1024]{1,0:T(8,128)}), f32[896,1024]{1,0:T(8,128)}) %all-reduce.4.cloned.1.call-update) | async-done | bytes 3670032
  2063.4 1.5 fusion.53
  (21 shorter events, 0.1 us)
Async XLA Ops:
  7.2 15.8 copy-start
  7.2 2.8 copy-start.10
  7.2 5.2 copy-start.11
  7.2 8.2 copy-start.9
  7.2 13.0 copy-start.5
  7.2 2056.1 %all-reduce.4.cloned.1.call-start = ((), (), s32[]{:S(2)}) async-start(), calls=%async_computation | async-start | bytes 7340032
  8.6 9.7 collective-permute-start
  10.6 6.5 collective-permute-start.2
  12.4 6.0 collective-permute-start.1
  18.4 0.8 copy-start.8
  22.9 2.2 copy-start.3
  23.8 5.4 copy-start.1
  23.8 1.3 copy-start.7
  38.9 1.2 copy-start.6
  40.8 4.4 copy-start.4
  41.9 5.2 copy-start.2
  41.9 24.8 %collective-permute-start.3 = (f32[1,256,896]{2,1,0:T(8,128)S(1)}, f32[1,256,896]{2,1,0:T(8,128)}, u32[]{:S(2)}, u32[]{:S(2)}) collective-permute-start(f32[1,256,896]{2,1,0:T(8,128)S(1)} %get-tuple-element.10), channel_id=1, source_target_pairs={{4,0},{8,4},{12,8},{16,12},{20,16},{24,20},{28,24},{32,28},{36,32}... | collective-permute-start | bytes 2752520 | tf_op jit(solution)/shard_map/ppermute | solution.py:16
Sparse Core Ops, SparseCore 0:
  39.0 2024.3 all-reduce.3
where the time goes:
time: 2070 us
  waiting for transfers between devices  1890 us (91%)
  blocking collectives  116 us (6%)
  matrix products  20.9 us (1%)
    unnamed x2, waiting for transfers between devices  1880 us
    psum x1, blocking collectives, shards(): grad_rows = lax.psum(partial_sum, 'tensor').astype(jnp.bfloat16)  116 us
  transfers between devices with their start and end apart: 5, of which 2 were waited for; matrix products, arithmetic and copies ran while one was open for 1% of the time, Pallas kernels for 0%

commit v1 on v0

v1 whole, which is shorter than its diff:
```python
import functools

import jax
import jax.numpy as jnp
import numpy as np
from jax import lax
from jax.experimental import pallas as pl
from jax.experimental.pallas import tpu as pltpu
from jax.sharding import Mesh, PartitionSpec as P

HEAD_DIM = 128
STRETCH = 64
BF16 = jnp.bfloat16
F32 = jnp.float32

masked_score = -1e30


def matmul(left, right, left_dim, right_dim):
    contracted = (((left_dim,), (right_dim,)), ((), ()))
    return lax.dot_general(left, right, contracted, preferred_element_type=F32)


def attend(encodings, key_weight, value_weight, usable, gate, queries, grad_out, out):
    attended, grad_queries, grad_keys, grad_values = out
    score_scale = HEAD_DIM ** (-0.5)
    keys_all = matmul(encodings, key_weight[...], 1, 0).astype(BF16)
    values_all = matmul(encodings, value_weight[...], 1, 0).astype(BF16)
    gated_all = jnp.where(gate, grad_out, jnp.zeros_like(grad_out))
    for head in range(queries.shape[1] // HEAD_DIM):
        span = slice(head * HEAD_DIM, (head + 1) * HEAD_DIM)
        query, grad = queries[:, span], gated_all[:, span]
        keys, values = keys_all[:, span], values_all[:, span]
        scores = jnp.where(usable, matmul(query, keys, 1, 1) * score_scale, masked_score)
        raised = jnp.exp(scores - jnp.max(scores, axis=-1, keepdims=True))
        weights = raised / jnp.sum(raised, axis=-1, keepdims=True)
        weights_half = weights.astype(BF16)
        mixed = matmul(weights_half, values, 1, 0)
        attended[:, span] = jnp.where(gate, mixed, 0.0).astype(BF16)
        grad_weights = matmul(grad, values, 1, 1)
        inner = jnp.sum(weights * grad_weights, axis=-1, keepdims=True)
        grad_scores = (weights * (grad_weights - inner) * score_scale).astype(BF16)
        grad_queries[:, span] = matmul(grad_scores, keys, 1, 0).astype(BF16)
        grad_keys[:, span] = matmul(grad_scores, query, 0, 0).astype(BF16)
        grad_values[:, span] = matmul(weights_half, grad, 0, 0).astype(BF16)


def encoding_partials(core, key_weight, value_weight, grad_keys, grad_values, kept, sent):
    half = kept.shape[0]

    def partial_of(part):
        rows = pl.ds(pl.multiple_of(part * half, half), half)
        return matmul(grad_keys[rows, :], key_weight[...], 1, 1) + matmul(
            grad_values[rows, :], value_weight[...], 1, 1
        )

    sent[...] = partial_of(1 - core).astype(BF16)
    kept[...] = partial_of(core)


def own_pair(facts, neighbours, key_weight, value_weight, ids, queries, grad_out, *out):
    attended, grad_queries, grad_keys, grad_values, kept, sent = out
    gate = jnp.full((1, 1), facts[0], jnp.int32) == facts[1]
    attend(
        neighbours[0], key_weight, value_weight, ids[0:1, :] != 0, gate,
        queries[STRETCH:, :], grad_out[STRETCH:, :],
        (attended, grad_queries, grad_keys, grad_values),
    )
    encoding_partials(facts[2], key_weight, value_weight, grad_keys, grad_values, kept, sent)


def next_pair(facts, neighbours, key_weight, value_weight, ids, payload, first_keys, first_values, *out):
    answer, kept, sent, weight_grad, grad_keys, grad_values = out
    document = payload[2 * STRETCH:2 * STRETCH + 1, 0:1].astype(F32)
    follows = jnp.full((1, 1), facts[3], jnp.int32) == 1
    gate = jnp.logical_and(document == facts[1].astype(F32), follows)
    attend(
        neighbours[1], key_weight, value_weight, ids[1:2, :] != 0, gate,
        payload[0:STRETCH, :], payload[STRETCH:2 * STRETCH, :],
        (answer.at[0:STRETCH], answer.at[STRETCH:2 * STRETCH], grad_keys, grad_values),
    )
    encoding_partials(facts[2], key_weight, value_weight, grad_keys, grad_values, kept, sent)
    width = grad_keys.shape[1]
    for side, (first, second) in enumerate(((first_keys, grad_keys), (first_values, grad_values))):
        total = matmul(neighbours[0], first[...], 0, 0) + matmul(neighbours[1], second[...], 0, 0)
        weight_grad[:, side * width:(side + 1) * width] = total.astype(BF16)


def call(kernel, out_shapes, scratch, flops, moved):
    vmem = pl.BlockSpec(memory_space=pltpu.VMEM)
    smem = pl.BlockSpec(memory_space=pltpu.SMEM)

    def run(facts, *arrays):
        return pl.pallas_call(
            kernel,
            out_shape=[jax.ShapeDtypeStruct(s, d) for s, d in out_shapes],
            in_specs=[smem] + [vmem] * len(arrays),
            out_specs=[vmem] * len(out_shapes),
            scratch_shapes=[pltpu.VMEM(s, d) for s, d in scratch],
            compiler_params=pltpu.CompilerParams(vmem_limit_bytes=48 * 2**20),
            cost_estimate=pl.CostEstimate(flops=flops, bytes_accessed=moved, transcendentals=65536),
        )(facts, *arrays)

    return run


def swap(block, axis):
    return lax.ppermute(block, axis, [(0, 1), (1, 0)])


def shards(queries, neighbours, key_weight, value_weight, neighbour_ids, block_document, grad_out):
    tokens, width = queries.shape[1:]
    slots, enc_width = neighbours.shape[2:]
    half = slots // 2
    run_count = lax.axis_size("y") * lax.axis_size("z")
    run_index = lax.axis_index(("y", "z"))
    documents = block_document[0]
    facts = jnp.stack(
        [
            documents[0],
            documents[1],
            lax.axis_index("c").astype(jnp.int32),
            (run_index < run_count - 1).astype(jnp.int32),
        ]
    )
    document_rows = jnp.broadcast_to(documents[0].astype(BF16), (16, width))
    payload = jnp.concatenate(
        [queries[0, :STRETCH], grad_out[0, :STRETCH], document_rows], axis=0
    )
    payload = lax.ppermute(payload, ("y", "z"), [(i, i - 1) for i in range(1, run_count)])

    pair_out = [
        ((STRETCH, width), BF16),
        ((STRETCH, width), BF16),
        ((slots, width), BF16),
        ((slots, width), BF16),
        ((half, enc_width), F32),
        ((half, enc_width), BF16),
    ]
    attended, grad_queries, first_keys, first_values, kept_a, sent_a = call(
        own_pair, pair_out, [], 1_100_000_000, 4_000_000
    )(facts, neighbours[0], key_weight, value_weight, neighbour_ids[0], queries[0], grad_out[0])
    got_a = swap(sent_a, "c")

    next_out = [
        ((2 * STRETCH, width), BF16),
        ((half, enc_width), F32),
        ((half, enc_width), BF16),
        ((enc_width, 2 * width), BF16),
    ]
    answer, kept_b, sent_b, weight_grad = call(
        next_pair, next_out, [((slots, width), BF16)] * 2, 2_000_000_000, 6_000_000
    )(facts, neighbours[0], key_weight, value_weight, neighbour_ids[0], payload, first_keys, first_values)
    got_b = swap(sent_b, "c")

    chip_a = (kept_a + got_a.astype(F32)).astype(BF16)
    far_a = swap(chip_a, "h")
    chip_b = (kept_b + got_b.astype(F32)).astype(BF16)
    far_b = swap(chip_b, "h")

    answer = lax.ppermute(answer, ("y", "z"), [(i - 1, i) for i in range(1, run_count)])
    attended = jnp.concatenate([answer[:STRETCH], attended], axis=0)
    grad_queries = jnp.concatenate([answer[STRETCH:], grad_queries], axis=0)

    groups = lax.axis_size("x") * lax.axis_size("y")
    depth = lax.axis_size("z")
    terms = lax.all_to_all(weight_grad, ("x", "y"), 0, 0, tiled=True)
    rows = jnp.sum(terms.reshape(groups, enc_width // groups, 2 * width).astype(F32), axis=0)
    rows = rows.reshape(depth, -1, 2 * width)
    own_rows = rows.shape[1]
    rows = jnp.pad(rows, ((0, 0), (0, 8 - own_rows), (0, 0)))
    rows = lax.all_to_all(rows, "z", 0, 0, tiled=True)
    weight_rows = jnp.sum(rows, axis=0)[:own_rows]

    half_a = (chip_a.astype(F32) + far_a.astype(F32)).astype(BF16)
    half_b = (chip_b.astype(F32) + far_b.astype(F32)).astype(BF16)
    grad_rows = jnp.stack(
        [
            lax.all_gather(half_a, "c", axis=0, tiled=True),
            lax.all_gather(half_b, "c", axis=0, tiled=True),
        ]
    )
    return (
        attended[None],
        grad_queries[None],
        grad_rows[None],
        weight_rows[:, :width],
        weight_rows[:, width:],
    )


def solution(mesh):
    chips = Mesh(np.asarray(mesh.devices).reshape(4, 4, 8, 2, 2), ("x", "y", "z", "h", "c"))
    runs, heads = ("y", "z"), ("h", "c")
    in_specs = (
        P("x", runs, heads),
        P("x", runs, None, None),
        P(None, heads),
        P(None, heads),
        P("x", runs, None),
        P("x", runs),
        P("x", runs, heads),
    )
    out_specs = (
        P("x", runs, heads),
        P("x", runs, heads),
        P("x", runs, None, None),
        P(("x", "y", "z"), heads),
        P(("x", "y", "z"), heads),
    )
    return jax.shard_map(shards, mesh=chips, in_specs=in_specs, out_specs=out_specs, check_vma=False)
```

time: 2070 us -> 121 us (0.06)
  the two profiles are of different devices: /device:TPU:0 before, /device:TPU:137 now
where the time goes in v1:
time: 121 us; the launch traced here: 120 us
  starting transfers between devices  55.8 us (46%)
  waiting for transfers between devices  23 us (19%)
  blocking collectives  13.6 us (11%)
  local copies, waits for them, and re-layouts  10.4 us (9%)
  Pallas kernels  10.4 us (9%)
  other arithmetic  5.27 us (4%)
  between operations  1.45 us (1%)
    all_to_all x1, starting transfers between devices, shards(): rows = lax.all_to_all(rows, 'z', 0, 0, tiled=True)  23 us
    ppermute x4, waiting for transfers between devices, swap(): return lax.ppermute(block, axis, [(0, 1), (1, 0)])  21.2 us
    ppermute x4, starting transfers between devices, swap(): return lax.ppermute(block, axis, [(0, 1), (1, 0)])  20.5 us
    all_gather x1, blocking collectives, shards(): lax.all_gather(half_a, 'c', axis=0, tiled=True)  10.5 us
    pallas_call x2, Pallas kernels, run(): pl.pallas_call(kernel, out_shape=[jax.ShapeDtypeStruct(s, d) for s, d in...  10.4 us
    all_to_all x1, starting transfers between devices, shards(): terms = lax.all_to_all(weight_grad, ('x', 'y'), 0, 0, tiled=True)  6.83 us
    unnamed x12, local copies, waits for them, and re-layouts  6.03 us
    ppermute x1, starting transfers between devices, shards(): lax.ppermute(answer, ('y', 'z'), [(i - 1, i) for i in range(1, run_count)])  3.55 us
  transfers between devices with their start and end apart: 8, of which 2 were waited for; matrix products, arithmetic and copies ran while one was open for 5% of the time, Pallas kernels for 3%

profile of v1, /device:TPU:137, one launch (start us, length us, event | category | flops | bytes accessed | tf_op | source)
XLA Modules:
  0.0 119.9 jit_solution(14677954261461741056)
XLA Ops:
  0.6 1.3 %fusion.2 = (s32[1,1]{1,0:T(1,128)}, s32[1,1]{1,0:T(1,128)}) fusion(s32[1,2]{1,0:T(1,128)} %param.12), kind=kLoop, calls=%fused_computation.14 | loop fusion | bytes 16 | tf_op jit(solution)/shard_map/slice | solution.py:120
  2.6 0.8 slice_bitcast_fusion
  3.4 0.8 slice_bitcast_fusion.1
  4.3 0.1 maximum_maximum_fusion
  4.4 1.9 %collective-permute-start = (bf16[144,512]{1,0:T(8,128)(2,1)S(1)}, bf16[144,512]{1,0:T(8,128)(2,1)S(1)}, u32[]{:S(2)}, u32[]{:S(2)}) collective-permute-start(bf16[144,512]{1,0:T(8,128)(2,1)S(1)} %maximum_maximum_fusion), channel_id=1, source_target_pairs={{4,0},{8,4},{12,8},{16,12},{20,16},{24,20},{28,24},{32,28},{36,32}... | collective-permute-start | bytes 442376 | tf_op jit(solution)/shard_map/ppermute | solution.py:130
  6.3 1.4 %pad_add_fusion.facts = s32[4]{0:T(128)S(1)} fusion(s32[1]{0:T(128)} %bitcast.3, s32[1]{0:T(128)} %bitcast.2, s32[1]{0:T(128)} %bitcast.1, s32[1]{0:T(128)} %bitcast), kind=kLoop, calls=%fused_computation.11 | loop fusion | flops 12 | bytes 32 | tf_op jit(solution)/shard_map/stack | solution.py:118
  7.7 0.0 copy-start
  7.7 0.9 copy-done
  8.6 0.0 copy-start.1
  8.6 0.9 copy-done.1
  9.5 0.0 copy-start.2
  9.5 1.2 copy-done.2
  10.7 0.0 copy-start.3
  10.7 1.2 copy-done.3
  11.9 0.0 copy-start.4
  11.9 1.2 copy-done.4
  13.1 0.0 copy-start.5
  13.1 0.7 copy-done.5
  13.7 4.1 %shard_map.110 = (bf16[64,512]{1,0:T(8,128)(2,1)S(1)}, bf16[64,512]{1,0:T(8,128)(2,1)S(1)}, bf16[256,512]{1,0:T(8,128)(2,1)S(1)}, bf16[256,512]{1,0:T(8,128)(2,1...) custom-call(s32[4]{0:T(128)S(1)} %pad_add_fusion.facts, bf16[2,256,896]{2,1,0:T(8,128)(2,1)S(1)} %bitcast.24, ...), custom_call_target="tpu_custom_call" | custom-call | flops 1100000000 | bytes 4000000 | tf_op jit(solution)/shard_map/pallas_call | solution.py:94
  17.8 0.0 collective-permute-done.payload
  17.9 6.3 %shard_map.111 = (bf16[128,512]{1,0:T(8,128)(2,1)S(1)}, f32[128,896]{1,0:T(8,128)S(1)}, bf16[128,896]{1,0:T(8,128)(2,1)S(1)}, bf16[896,1024]{1,0:T(8,128)(2,1)}) custom-call(s32[4]{0:T(128)S(1)} %pad_add_fusion.facts, bf16[2,256,896]{2,1,0:T(8,128)(2,1)S(1)} %bitcast.25, bf16[896,512]{1,0:T(8,128)(2,1)S(1)} %copy-done.3, bf16[896,512]{1,0:T(8,128)(2,1)S(1)} %copy-done.4, ...), custom_call_target="tpu_custom_call" | custom-call | flops 2000000000 | bytes 6000000 | tf_op jit(solution)/shard_map/pallas_call | solution.py:94
  24.2 6.8 %all-to-all-start = ((bf16[16,56,1024]{2,1,0:T(8,128)(2,1)}), bf16[16,56,1024]{2,1,0:T(8,128)(2,1)}, u32[]{:S(2)}, u32[]{:S(2)}) async-start(bf16[16,56,1024]{2,1,0:T(8,128)(2,1)} %bitcast.16), calls=%async_computation | async-start | bytes 3670016 | tf_op jit(solution)/shard_map/all_to_all | solution.py:167
  31.0 3.2 %collective-permute-start.2 = (bf16[128,896]{1,0:T(8,128)(2,1)S(1)}, bf16[128,896]{1,0:T(8,128)(2,1)S(1)}, u32[]{:S(2)}, u32[]{:S(2)}) collective-permute-start(bf16[128,896]{1,0:T(8,128)(2,1)S(1)} %get-tuple-element.21), channel_id=1, source_target_pairs={{0,1},{1,0},{2,3},{3,2},{4,5},{5,4},{6,7},{7,6},{8,9},{9,8},{10,11... | collective-permute-start | bytes 688136 | tf_op jit(solution)/shard_map/ppermute | solution.py:108
  34.2 1.9 %collective-permute-start.4 = (bf16[128,896]{1,0:T(8,128)(2,1)S(1)}, bf16[128,896]{1,0:T(8,128)(2,1)S(1)}, u32[]{:S(2)}, u32[]{:S(2)}) collective-permute-start(bf16[128,896]{1,0:T(8,128)(2,1)S(1)} %get-tuple-element.23), channel_id=1, source_target_pairs={{0,1},{1,0},{2,3},{3,2},{4,5},{5,4},{6,7},{7,6},{8,9},{9,8},{10,11... | collective-permute-start | bytes 688136 | tf_op jit(solution)/shard_map/ppermute | solution.py:108
  36.2 3.5 %collective-permute-start.1 = (bf16[128,512]{1,0:T(8,128)(2,1)S(1)}, bf16[128,512]{1,0:T(8,128)(2,1)S(1)}, u32[]{:S(2)}, u32[]{:S(2)}) collective-permute-start(bf16[128,512]{1,0:T(8,128)(2,1)S(1)} %get-tuple-element.17), channel_id=1, source_target_pairs={{0,4},{4,8},{8,12},{12,16},{16,20},{20,24},{24,28},{28,32},{32,36}... | collective-permute-start | bytes 393224 | tf_op jit(solution)/shard_map/ppermute | solution.py:161
  39.7 0.0 collective-permute-done.2
  39.7 0.1 add_convert_fusion.3
  39.8 11.1 %collective-permute-start.3 = (bf16[128,896]{1,0:T(8,128)(2,1)S(1)}, bf16[128,896]{1,0:T(8,128)(2,1)S(1)}, u32[]{:S(2)}, u32[]{:S(2)}) collective-permute-start(bf16[128,896]{1,0:T(8,128)(2,1)S(1)} %add_convert_fusion.3), channel_id=1, source_target_pairs={{0,2},{2,0},{1,3},{3,1},{4,6},{6,4},{5,7},{7,5},{8,10},{10,8},{9,1... | collective-permute-start | bytes 688136 | tf_op jit(solution)/shard_map/ppermute | solution.py:108
  50.9 0.0 collective-permute-done.1
  50.9 0.7 maximum_bitcast_fusion.1
  51.7 1.8 %all-to-all-done = bf16[16,56,1024]{2,1,0:T(8,128)(2,1)} async-done(((bf16[16,56,1024]{2,1,0:T(8,128)(2,1)}), bf16[16,56,1024]{2,1,0:T(8,128)(2,1)}, u32[]{:S(2)}, u32[]{:S(2)}) %all-to-all-start) | async-done | bytes 1835040 | tf_op jit(solution)/shard_map/all_to_all | solution.py:167
  53.5 1.9 %convert_reduce_fusion = f32[56,1024]{1,0:T(8,128)S(1)} fusion(bf16[16,56,1024]{2,1,0:T(8,128)(2,1)} %all-to-all-done), kind=kLoop, calls=%fused_computation | loop fusion | flops 1777664 | bytes 2064384 | tf_op jit(solution)/shard_map/reduce_sum | solution.py:168
  55.4 0.7 pad.4
  56.1 23.0 %all-to-all-start.1 = ((f32[8,8,1024]{2,1,0:T(8,128)}), f32[8,8,1024]{2,1,0:T(8,128)S(1)}, u32[]{:S(2)}, u32[]{:S(2)}) async-start(f32[8,8,1024]{2,1,0:T(8,128)} %pad.4), calls=%async_computation.1 | async-start | bytes 524288 | tf_op jit(solution)/shard_map/all_to_all | solution.py:172
  79.1 0.0 collective-permute-done.4
  79.2 4.2 %collective-permute-start.5 = (bf16[128,896]{1,0:T(8,128)(2,1)S(1)}, bf16[128,896]{1,0:T(8,128)(2,1)S(1)}, u32[]{:S(2)}, u32[]{:S(2)}) collective-permute-start(bf16[128,896]{1,0:T(8,128)(2,1)S(1)} %add_convert_fusion.1), channel_id=1, source_target_pairs={{0,2},{2,0},{1,3},{3,1},{4,6},{6,4},{5,7},{7,5},{8,10},{10,8},{9,1... | collective-permute-start | bytes 688136 | tf_op jit(solution)/shard_map/ppermute | solution.py:108
  83.4 0.0 collective-permute-done.3
  83.4 0.1 add_convert_fusion.2
  83.5 10.5 %all_gather.6 = bf16[256,896]{1,0:T(8,128)(2,1)S(1)} all-gather(bf16[128,896]{1,0:T(8,128)(2,1)S(1)} %add_convert_fusion.2), channel_id=1, replica_groups=mesh['x'=4,'y'=4,'z'=8,'h'=2,'c'=2] {'c'}, dimensions={0}, use_global_device_ids=true | all-gather | bytes 688128 | tf_op jit(solution)/shard_map/all_gather | solution.py:179
  93.9 21.2 %collective-permute-done.5 = bf16[128,896]{1,0:T(8,128)(2,1)S(1)} collective-permute-done((bf16[128,896]{1,0:T(8,128)(2,1)S(1)}, bf16[128,896]{1,0:T(8,128)(2,1)S(1)}, u32[]{:S(2)}, u32[]{:S(2)}) %collective-permute-start.5) | collective-permute-done | bytes 229408 | tf_op jit(solution)/shard_map/ppermute | solution.py:108
  115.1 0.1 add_convert_fusion
  115.1 3.1 %all_gather.7 = bf16[256,896]{1,0:T(8,128)(2,1)S(1)} all-gather(bf16[128,896]{1,0:T(8,128)(2,1)S(1)} %add_convert_fusion), channel_id=1, replica_groups=mesh['x'=4,'y'=4,'z'=8,'h'=2,'c'=2] {'c'}, dimensions={0}, use_global_device_ids=true | all-gather | bytes 688128 | tf_op jit(solution)/shard_map/all_gather | solution.py:180
  118.3 1.0 maximum_bitcast_fusion
  119.3 0.0 all-to-all-done.1
  119.3 0.6 fusion.1
  (6 shorter events, 0.1 us)
Async XLA Ops:
  4.4 13.4 %collective-permute-start = (bf16[144,512]{1,0:T(8,128)(2,1)S(1)}, bf16[144,512]{1,0:T(8,128)(2,1)S(1)}, u32[]{:S(2)}, u32[]{:S(2)}) collective-permute-start(bf16[144,512]{1,0:T(8,128)(2,1)S(1)} %maximum_maximum_fusion), channel_id=1, source_target_pairs={{4,0},{8,4},{12,8},{16,12},{20,16},{24,20},{28,24},{32,28},{36,32}... | collective-permute-start | bytes 442376 | tf_op jit(solution)/shard_map/ppermute | solution.py:130
  7.7 0.9 copy-start
  8.6 0.9 copy-start.1
  9.5 1.2 copy-start.2
  10.7 1.2 copy-start.3
  11.9 1.2 copy-start.4
  13.1 0.7 copy-start.5
  24.2 29.3 %all-to-all-start = ((bf16[16,56,1024]{2,1,0:T(8,128)(2,1)}), bf16[16,56,1024]{2,1,0:T(8,128)(2,1)}, u32[]{:S(2)}, u32[]{:S(2)}) async-start(bf16[16,56,1024]{2,1,0:T(8,128)(2,1)} %bitcast.16), calls=%async_computation | async-start | bytes 3670016 | tf_op jit(solution)/shard_map/all_to_all | solution.py:167
  31.0 8.7 %collective-permute-start.2 = (bf16[128,896]{1,0:T(8,128)(2,1)S(1)}, bf16[128,896]{1,0:T(8,128)(2,1)S(1)}, u32[]{:S(2)}, u32[]{:S(2)}) collective-permute-start(bf16[128,896]{1,0:T(8,128)(2,1)S(1)} %get-tuple-element.21), channel_id=1, source_target_pairs={{0,1},{1,0},{2,3},{3,2},{4,5},{5,4},{6,7},{7,6},{8,9},{9,8},{10,11... | collective-permute-start | bytes 688136 | tf_op jit(solution)/shard_map/ppermute | solution.py:108
  34.2 44.9 %collective-permute-start.4 = (bf16[128,896]{1,0:T(8,128)(2,1)S(1)}, bf16[128,896]{1,0:T(8,128)(2,1)S(1)}, u32[]{:S(2)}, u32[]{:S(2)}) collective-permute-start(bf16[128,896]{1,0:T(8,128)(2,1)S(1)} %get-tuple-element.23), channel_id=1, source_target_pairs={{0,1},{1,0},{2,3},{3,2},{4,5},{5,4},{6,7},{7,6},{8,9},{9,8},{10,11... | collective-permute-start | bytes 688136 | tf_op jit(solution)/shard_map/ppermute | solution.py:108
  36.2 14.8 %collective-permute-start.1 = (bf16[128,512]{1,0:T(8,128)(2,1)S(1)}, bf16[128,512]{1,0:T(8,128)(2,1)S(1)}, u32[]{:S(2)}, u32[]{:S(2)}) collective-permute-start(bf16[128,512]{1,0:T(8,128)(2,1)S(1)} %get-tuple-element.17), channel_id=1, source_target_pairs={{0,4},{4,8},{8,12},{12,16},{16,20},{20,24},{24,28},{28,32},{32,36}... | collective-permute-start | bytes 393224 | tf_op jit(solution)/shard_map/ppermute | solution.py:161
  39.8 43.6 %collective-permute-start.3 = (bf16[128,896]{1,0:T(8,128)(2,1)S(1)}, bf16[128,896]{1,0:T(8,128)(2,1)S(1)}, u32[]{:S(2)}, u32[]{:S(2)}) collective-permute-start(bf16[128,896]{1,0:T(8,128)(2,1)S(1)} %add_convert_fusion.3), channel_id=1, source_target_pairs={{0,2},{2,0},{1,3},{3,1},{4,6},{6,4},{5,7},{7,5},{8,10},{10,8},{9,1... | collective-permute-start | bytes 688136 | tf_op jit(solution)/shard_map/ppermute | solution.py:108
  56.1 63.2 %all-to-all-start.1 = ((f32[8,8,1024]{2,1,0:T(8,128)}), f32[8,8,1024]{2,1,0:T(8,128)S(1)}, u32[]{:S(2)}, u32[]{:S(2)}) async-start(f32[8,8,1024]{2,1,0:T(8,128)} %pad.4), calls=%async_computation.1 | async-start | bytes 524288 | tf_op jit(solution)/shard_map/all_to_all | solution.py:172
  79.2 35.9 %collective-permute-start.5 = (bf16[128,896]{1,0:T(8,128)(2,1)S(1)}, bf16[128,896]{1,0:T(8,128)(2,1)S(1)}, u32[]{:S(2)}, u32[]{:S(2)}) collective-permute-start(bf16[128,896]{1,0:T(8,128)(2,1)S(1)} %add_convert_fusion.1), channel_id=1, source_target_pairs={{0,2},{2,0},{1,3},{3,1},{4,6},{6,4},{5,7},{7,5},{8,10},{10,8},{9,1... | collective-permute-start | bytes 688136 | tf_op jit(solution)/shard_map/ppermute | solution.py:108

commit v2 on v1

v2 whole, which is shorter than its diff:
```python
import functools

import jax
import jax.numpy as jnp
import numpy as np
from jax import lax
from jax.experimental import pallas as pl
from jax.experimental.pallas import tpu as pltpu
from jax.sharding import Mesh, PartitionSpec as P

HEAD_DIM = 128
STRETCH = 64
BF16 = jnp.bfloat16
F32 = jnp.float32

masked_score = -1e30


def matmul(left, right, left_dim, right_dim):
    contracted = (((left_dim,), (right_dim,)), ((), ()))
    return lax.dot_general(left, right, contracted, preferred_element_type=F32)


def project(encodings, weight):
    return matmul(encodings, weight[...], 1, 0).astype(BF16)


def attend(keys_all, values_all, usable, gate, queries, grad_out, out):
    attended, grad_queries, grad_keys, grad_values = out
    score_scale = HEAD_DIM ** (-0.5)
    gated_all = jnp.where(gate, grad_out, jnp.zeros_like(grad_out))
    for head in range(queries.shape[1] // HEAD_DIM):
        span = slice(head * HEAD_DIM, (head + 1) * HEAD_DIM)
        query, grad = queries[:, span], gated_all[:, span]
        keys, values = keys_all[:, span], values_all[:, span]
        scores = jnp.where(usable, matmul(query, keys, 1, 1) * score_scale, masked_score)
        raised = jnp.exp(scores - jnp.max(scores, axis=-1, keepdims=True))
        weights = raised / jnp.sum(raised, axis=-1, keepdims=True)
        weights_half = weights.astype(BF16)
        mixed = matmul(weights_half, values, 1, 0)
        attended[:, span] = jnp.where(gate, mixed, 0.0).astype(BF16)
        grad_weights = matmul(grad, values, 1, 1)
        inner = jnp.sum(weights * grad_weights, axis=-1, keepdims=True)
        grad_scores = (weights * (grad_weights - inner) * score_scale).astype(BF16)
        grad_queries[:, span] = matmul(grad_scores, keys, 1, 0).astype(BF16)
        grad_keys[:, span] = matmul(grad_scores, query, 0, 0).astype(BF16)
        grad_values[:, span] = matmul(weights_half, grad, 0, 0).astype(BF16)


def encoding_partials(core, key_weight, value_weight, grad_keys, grad_values, kept, sent):
    half = kept.shape[0]

    def partial_of(part):
        rows = pl.ds(pl.multiple_of(part * half, half), half)
        return matmul(grad_keys[rows, :], key_weight[...], 1, 1) + matmul(
            grad_values[rows, :], value_weight[...], 1, 1
        )

    sent[...] = partial_of(1 - core).astype(BF16)
    kept[...] = partial_of(core)


def load(documents_in, ids_in, neighbours_in, key_in, value_in, queries_in, grad_in, *rest):
    payload, documents, ids, neighbours, key_weight, value_weight, queries, grad_out, sems = rest
    moves = (
        (documents_in, documents),
        (queries_in.at[0, 0:STRETCH], payload.at[0:STRETCH]),
        (grad_in.at[0, 0:STRETCH], payload.at[STRETCH:2 * STRETCH]),
        (neighbours_in.at[0], neighbours),
        (key_in, key_weight),
        (value_in, value_weight),
        (queries_in.at[0, STRETCH:2 * STRETCH], queries),
        (grad_in.at[0, STRETCH:2 * STRETCH], grad_out),
        (ids_in.at[0], ids),
    )
    copies = [pltpu.make_async_copy(*move, sems.at[i]) for i, move in enumerate(moves)]
    for copy in copies:
        copy.start()
    copies[0].wait()
    first = documents[0:1, 0:1].astype(F32)
    payload[2 * STRETCH:, :] = jnp.broadcast_to(first, (16, payload.shape[1])).astype(BF16)
    for copy in copies[1:]:
        copy.wait()


def own_pair(documents, ids, neighbours, key_weight, value_weight, queries, grad_out, *out):
    attended, grad_queries, grad_keys, grad_values, kept, sent, next_keys, next_values = out
    gate = documents[0:1, 0:1] == documents[0:1, 1:2]
    attend(
        project(neighbours[0], key_weight), project(neighbours[0], value_weight),
        ids[0:1, :] != 0, gate,
        queries[...], grad_out[...], (attended, grad_queries, grad_keys, grad_values),
    )
    encoding_partials(lax.axis_index("c"), key_weight, value_weight, grad_keys, grad_values, kept, sent)
    next_keys[...] = project(neighbours[1], key_weight)
    next_values[...] = project(neighbours[1], value_weight)


def next_pair(
    documents, ids, key_weight, value_weight, keys, values, payload, kept_a, sent_a, *out
):
    answer, grad_keys, grad_values, kept, sent = out
    kept[0] = kept_a[...]
    sent[0] = sent_a[...]
    last_run = lax.axis_size("y") * lax.axis_size("z") - 1
    run = lax.axis_index("y") * lax.axis_size("z") + lax.axis_index("z")
    follows = jnp.full((1, 1), run, jnp.int32) < last_run
    document = payload[2 * STRETCH:2 * STRETCH + 1, 0:1].astype(F32)
    gate = jnp.logical_and(document == documents[0:1, 1:2].astype(F32), follows)
    attend(
        keys[...], values[...], ids[1:2, :] != 0, gate,
        payload[0:STRETCH, :], payload[STRETCH:2 * STRETCH, :],
        (answer.at[0:STRETCH], answer.at[STRETCH:2 * STRETCH], grad_keys, grad_values),
    )
    encoding_partials(lax.axis_index("c"), key_weight, value_weight, grad_keys, grad_values, kept.at[1], sent.at[1])


def weight_partial(neighbours, keys_a, keys_b, values_a, values_b, weight_grad):
    width = keys_a.shape[1]
    for side, (first, second) in enumerate(((keys_a, keys_b), (values_a, values_b))):
        total = matmul(neighbours[0], first[...], 0, 0) + matmul(neighbours[1], second[...], 0, 0)
        weight_grad[:, side * width:(side + 1) * width] = total.astype(BF16)


def join(weight_rows, answer, second_attended, second_queries, attended, grad_queries):
    attended[0, 0:STRETCH, :] = answer[0:STRETCH, :]
    attended[0, STRETCH:, :] = second_attended[...]
    grad_queries[0, 0:STRETCH, :] = answer[STRETCH:, :]
    grad_queries[0, STRETCH:, :] = second_queries[...]


def add_cores(kept, got, weight_grad, chip_sum):
    chip_sum[...] = (kept[...] + got[...].astype(F32)).astype(BF16)


def finish(near, far, weight_rows, halves):
    halves[...] = (near[...].astype(F32) + far[...].astype(F32)).astype(BF16)


def call(kernel, out_shapes, flops, moved, space=pltpu.VMEM, scratch=()):
    def run(*arrays):
        if space == pltpu.HBM:
            arrays = [pltpu.with_memory_space_constraint(a, pltpu.HBM) for a in arrays]
        return pl.pallas_call(
            kernel,
            out_shape=[jax.ShapeDtypeStruct(s, d) for s, d in out_shapes],
            in_specs=[pl.BlockSpec(memory_space=space)] * len(arrays),
            out_specs=[pl.BlockSpec(memory_space=pltpu.VMEM)] * len(out_shapes),
            scratch_shapes=list(scratch),
            compiler_params=pltpu.CompilerParams(vmem_limit_bytes=48 * 2**20),
            cost_estimate=pl.CostEstimate(flops=flops, bytes_accessed=moved, transcendentals=0),
        )(*arrays)

    return run


def swap(block, axis):
    return lax.ppermute(block, axis, [(0, 1), (1, 0)])


def scatter_sum(rows, axis):
    index = lax.axis_index(axis)
    count = lax.axis_size(axis)
    step = 1
    while step < count:
        pairs = rows.reshape(rows.shape[0] // 2, 2, *rows.shape[1:])
        upper = (index // step) % 2 == 1
        sent = jnp.where(upper, pairs[:, 0], pairs[:, 1])
        kept = jnp.where(upper, pairs[:, 1], pairs[:, 0])
        rows = kept + lax.ppermute(sent, axis, [(i, i ^ step) for i in range(count)])
        step *= 2
    return rows[0]


def shards(queries, neighbours, key_weight, value_weight, neighbour_ids, block_document, grad_out):
    tokens, width = queries.shape[1:]
    slots, enc_width = neighbours.shape[2:]
    half = slots // 2
    run_count = lax.axis_size("y") * lax.axis_size("z")
    half_rows = [((half, enc_width), F32), ((half, enc_width), BF16)]
    payload, documents, ids, encodings, key_local, value_local, second_queries, second_grad = call(
        load,
        [
            ((2 * STRETCH + 16, width), BF16),
            (block_document.shape, jnp.int32),
            (neighbour_ids.shape[1:], jnp.int32),
            (neighbours.shape[1:], BF16),
            (key_weight.shape, BF16),
            (value_weight.shape, BF16),
            ((STRETCH, width), BF16),
            ((STRETCH, width), BF16),
        ],
        0,
        6_000_000,
        space=pltpu.HBM,
        scratch=[pltpu.SemaphoreType.DMA((9,))],
    )(block_document, neighbour_ids, neighbours, key_weight, value_weight, queries, grad_out)
    payload = lax.ppermute(payload, ("y", "z"), [(i, i - 1) for i in range(1, run_count)])

    attended, grad_queries, keys_a, values_a, kept_a, sent_a, next_keys, next_values = call(
        own_pair,
        [((STRETCH, width), BF16)] * 2
        + [((slots, width), BF16)] * 2
        + half_rows
        + [((slots, width), BF16)] * 2,
        1_100_000_000,
        10_000_000,
    )(documents, ids, encodings, key_local, value_local, second_queries, second_grad)

    answer, keys_b, values_b, kept, sent = call(
        next_pair,
        [((2 * STRETCH, width), BF16)]
        + [((slots, width), BF16)] * 2
        + [((2, half, enc_width), F32), ((2, half, enc_width), BF16)],
        1_100_000_000,
        10_000_000,
    )(
        documents, ids, key_local, value_local, next_keys, next_values, payload, kept_a, sent_a
    )
    got = swap(sent, "c")

    (weight_grad,) = call(
        weight_partial, [((enc_width, 2 * width), BF16)], 940_000_000, 6_000_000
    )(encodings, keys_a, keys_b, values_a, values_b)
    groups = lax.axis_size("x") * lax.axis_size("y")
    depth = lax.axis_size("z")
    (chip_sum,) = call(add_cores, [((2, half, enc_width), BF16)], 1_000_000, 2_000_000)(
        kept, got, weight_grad
    )
    far_sum = swap(chip_sum, "h")
    def sum_over_rows(partial):
        terms = lax.all_to_all(partial, ("x", "y"), 0, 0, tiled=True)
        rows = jnp.sum(terms.reshape(groups, enc_width // groups, 2 * width).astype(F32), axis=0)
        rows = rows.reshape(depth, -1, 2 * width)
        return jnp.pad(rows, ((0, 0), (0, 8 - rows.shape[1]), (0, 0))).astype(BF16)

    def sum_over_depth(rows):
        rows = lax.all_to_all(rows, "z", 0, 0, tiled=True)
        return jnp.sum(rows.astype(F32), axis=0)

    always = block_document[0, 0] >= 0
    rows = lax.cond(
        always,
        sum_over_rows,
        lambda partial: jnp.zeros((depth, 8, 2 * width), BF16),
        weight_grad,
    )
    answer, rows = lax.optimization_barrier((answer, rows))
    answer = lax.ppermute(answer, ("y", "z"), [(i - 1, i) for i in range(1, run_count)])
    weight_rows = lax.cond(
        always, sum_over_depth, lambda rows: jnp.zeros(rows.shape[1:], F32), rows
    )
    attended, grad_queries = call(join, [((1, tokens, width), BF16)] * 2, 1_000_000, 1_000_000)(
        weight_rows, answer, attended, grad_queries
    )

    (halves,) = call(finish, [((2, half, enc_width), BF16)], 1_000_000, 1_000_000)(
        chip_sum, far_sum, weight_rows
    )
    grad_rows = lax.all_gather(halves, "c", axis=1, tiled=True)
    weight_rows = weight_rows[:enc_width // groups // depth]
    return (
        attended,
        grad_queries,
        grad_rows[None],
        weight_rows[:, :width],
        weight_rows[:, width:],
    )


def solution(mesh):
    chips = Mesh(np.asarray(mesh.devices).reshape(4, 4, 8, 2, 2), ("x", "y", "z", "h", "c"))
    runs, heads = ("y", "z"), ("h", "c")
    in_specs = (
        P("x", runs, heads),
        P("x", runs, None, None),
        P(None, heads),
        P(None, heads),
        P("x", runs, None),
        P("x", runs),
        P("x", runs, heads),
    )
    out_specs = (
        P("x", runs, heads),
        P("x", runs, heads),
        P("x", runs, None, None),
        P(("x", "y", "z"), heads),
        P(("x", "y", "z"), heads),
    )
    return jax.shard_map(shards, mesh=chips, in_specs=in_specs, out_specs=out_specs, check_vma=False)
```

time: 121 us -> 98 us (0.81)
  the two profiles are of different devices: /device:TPU:137 before, /device:TPU:1 now
where the time goes in v2:
time: 98 us; the launch traced here: 97.7 us
  blocking collectives  59.9 us (61%)
  starting transfers between devices  22 us (22%)
  Pallas kernels  11.2 us (11%)
  waiting for transfers between devices  1.78 us (2%)
  local copies, waits for them, and re-layouts  1.61 us (2%)
    all_to_all x1, blocking collectives, sum_over_rows(): terms = lax.all_to_all(partial, ('x', 'y'), 0, 0, tiled=True)  33 us
    all_to_all x1, blocking collectives, sum_over_depth(): rows = lax.all_to_all(rows, 'z', 0, 0, tiled=True)  20.9 us
    ppermute x2, starting transfers between devices, swap(): return lax.ppermute(block, axis, [(0, 1), (1, 0)])  19.4 us
    pallas_call x7, Pallas kernels, run(): pl.pallas_call(kernel, out_shape=[jax.ShapeDtypeStruct(s, d) for s, d in...  11.2 us
    all_gather x1, blocking collectives, shards(): grad_rows = lax.all_gather(halves, 'c', axis=1, tiled=True)  5.99 us
  transfers between devices with their start and end apart: 4, of which 2 were waited for; matrix products, arithmetic and copies ran while one was open for 1% of the time, Pallas kernels for 6%

profile of v2, /device:TPU:1, one launch (start us, length us, event | category | flops | bytes accessed | tf_op | source)
XLA Modules:
  0.0 97.7 jit_solution(5089906159404267017)
XLA Ops:
  0.6 1.9 %shard_map.110 = (bf16[144,512]{1,0:T(8,128)(2,1)S(1)}, s32[1,2]{1,0:T(1,128)S(1)}, s32[2,256]{1,0:T(2,128)S(1)}, bf16[2,256,896]{2,1,0:T(8,128)(2,1)S(1)}, bf16...) custom-call(s32[1,2]{1,0:T(1,128)} %documents_in.1, ...), custom_call_target="tpu_custom_call" | custom-call | bytes 6000000 | tf_op jit(solution)/shard_map/pallas_call | solution.py:144
  2.6 1.3 %collective-permute-start = (bf16[144,512]{1,0:T(8,128)(2,1)S(1)}, bf16[144,512]{1,0:T(8,128)(2,1)S(1)}, u32[]{:S(2)}, u32[]{:S(2)}) collective-permute-start(bf16[144,512]{1,0:T(8,128)(2,1)S(1)} %get-tuple-element.47), channel_id=1, source_target_pairs={{4,0},{8,4},{12,8},{16,12},{20,16},{24,20},{28,24},{32,28},{36,32}... | collective-permute-start | bytes 442376 | tf_op jit(solution)/shard_map/ppermute | solution.py:198
  3.9 4.1 %shard_map.111 = (bf16[64,512]{1,0:T(8,128)(2,1)S(1)}, bf16[64,512]{1,0:T(8,128)(2,1)S(1)}, bf16[256,512]{1,0:T(8,128)(2,1)S(1)}, bf16[256,512]{1,0:T(8,128)(2,1...) custom-call(s32[1,2]{1,0:T(1,128)S(1)} %get-tuple-element.38.documen, ...), custom_call_target="tpu_custom_call" | custom-call | flops 1100000000 | bytes 10000000 | tf_op jit(solution)/shard_map/pallas_call | solution.py:144
  7.9 1.5 %collective-permute-done.payload = bf16[144,512]{1,0:T(8,128)(2,1)S(1)} collective-permute-done((bf16[144,512]{1,0:T(8,128)(2,1)S(1)}, bf16[144,512]{1,0:T(8,128)(2,1)S(1)}, u32[]{:S(2)}, u32[]{:S(2)}) %collective-permute-start) | collective-permute-done | bytes 147488 | tf_op jit(solution)/shard_map/ppermute | solution.py:198
  9.5 3.2 %shard_map.112 = (bf16[128,512]{1,0:T(8,128)(2,1)S(1)}, bf16[256,512]{1,0:T(8,128)(2,1)S(1)}, bf16[256,512]{1,0:T(8,128)(2,1)S(1)}, f32[2,128,896]{2,1,0:T(8,128)S(1)}, bf16[2,128,896]{2,1,0:T(8,128)(2,1)S(1)}) custom-call(s32[1,2]{1,0:T(1,128)S(1)} %get-tuple-element.38.documents, s32[2,256]{1,0:T(2,128)S(1)} %get-tuple-element.39.ids, ...), custom_call_target="tpu_custom_call" | custom-call | flops 1100000000 | bytes 10000000 | tf_op jit(solution)/shard_map/pallas_call | solution.py:144
  12.6 8.9 %collective-permute-start.2 = (bf16[2,128,896]{2,1,0:T(8,128)(2,1)S(1)}, bf16[2,128,896]{2,1,0:T(8,128)(2,1)S(1)}, u32[]{:S(2)}, u32[]{:S(2)}) collective-permute-start(bf16[2,128,896]{2,1,0:T(8,128)(2,1)S(1)} %get-tuple-element.62), channel_id=1, source_target_pairs={{0,1},{1,0},{2,3},{3,2},{4,5},{5,4},{6,7},{7,6},{8,9},{9,8},{10,11... | collective-permute-start | bytes 1376264 | tf_op jit(solution)/shard_map/ppermute | solution.py:158
  21.6 1.1 %shard_map.113.weight_grad = bf16[896,1024]{1,0:T(8,128)(2,1)S(1)} custom-call(bf16[2,256,896]{2,1,0:T(8,128)(2,1)S(1)} %get-tuple-element.42.neighbours, bf16[256,512]{1,0:T(8,128)(2,1)S(1)} %get-tuple-element.51.keys_a, bf16[256,512]{1,0:T(8,128)(2,1)S(1)} %get-tuple-element.52.keys_b, bf16[256,512]{1,0:T(8,128)(2,1)S(1)} %get-tuple-element.53.values_a, ...), custom_call_target="tpu_custom_call" | custom-call | flops 940000000 | bytes 6000000 | tf_op jit(solution)/shard_map/pallas_call | solution.py:144
  22.7 0.3 collective-permute-done.2.got
  23.0 0.0 copy-start
  23.0 0.1 shard_map.115.near
  23.1 10.5 %collective-permute-start.3 = (bf16[2,128,896]{2,1,0:T(8,128)(2,1)S(1)}, bf16[2,128,896]{2,1,0:T(8,128)(2,1)S(1)}, u32[]{:S(2)}, u32[]{:S(2)}) collective-permute-start(bf16[2,128,896]{2,1,0:T(8,128)(2,1)S(1)} %shard_map.115.near), channel_id=1, source_target_pairs={{0,2},{2,0},{1,3},{3,1},{4,6},{6,4},{5,7},{7,5},{8,10},{10,8},{9,1... | collective-permute-start | bytes 1376264 | tf_op jit(solution)/shard_map/ppermute | solution.py:158
  33.6 0.0 copy-done
  33.6 33.4 %conditional.2 = (bf16[8,8,1024]{2,1,0:T(8,128)(2,1)S(1)}) conditional(s32[]{:T(128)} %bitcast.1, () %tuple.22, bf16[896,1024]{1,0:T(8,128)(2,1)S(1)} %shard_map.113.weight_grad), branch_computations={%region_0.0_spmd, %region_1.3_spmd} | conditional | flops 860160 | bytes 6094860 | solution.py:242
  33.6 33.0 %all_to_all.11 = bf16[16,56,1024]{2,1,0:T(8,128)(2,1)S(1)} all-to-all(bf16[16,56,1024]{2,1,0:T(8,128)(2,1)S(1)} %bitcast.4), channel_id=1, replica_groups=mesh['x'=4,'y'=4,'z'=8,'h'=2,'c'=2] {'x','y'}, dimensions={0} | all-to-all | bytes 3670016 | tf_op jit(solution)/shard_map/cond/branch_1_fun/all_to_all | solution.py:232
  66.6 0.3 reduce
  67.0 1.3 %collective-permute-start.1 = (bf16[128,512]{1,0:T(8,128)(2,1)S(1)}, bf16[128,512]{1,0:T(8,128)(2,1)S(1)}, u32[]{:S(2)}, u32[]{:S(2)}) collective-permute-start(bf16[128,512]{1,0:T(8,128)(2,1)S(1)} %get-tuple-element.56), channel_id=1, source_target_pairs={{0,4},{4,8},{8,12},{12,16},{16,20},{20,24},{24,28},{28,32},{32,36}... | collective-permute-start | bytes 393224 | tf_op jit(solution)/shard_map/ppermute | solution.py:249
  68.3 21.0 %conditional.3 = (f32[8,1024]{1,0:T(8,128)S(1)}) conditional(s32[]{:T(128)} %bitcast.1, () %tuple.21, bf16[8,8,1024]{2,1,0:T(8,128)(2,1)S(1)} %get-tuple-element.75), branch_computations={%region_3.4_spmd, %region_4.6_spmd} | conditional | flops 122880 | bytes 425992 | solution.py:250
  68.4 20.9 %all_to_all.12 = bf16[8,8,1024]{2,1,0:T(8,128)(2,1)S(1)} all-to-all(bf16[8,8,1024]{2,1,0:T(8,128)(2,1)S(1)} %param.3), channel_id=1, replica_groups=mesh['x'=4,'y'=4,'z'=8,'h'=2,'c'=2] {'z'}, dimensions={0} | all-to-all | bytes 262144 | tf_op jit(solution)/shard_map/cond/branch_1_fun/all_to_all | solution.py:238
  89.3 0.6 fusion
  89.9 0.0 collective-permute-done.1.answer
  89.9 0.7 shard_map.114
  90.7 0.0 collective-permute-done.3.far
  90.7 0.1 shard_map.116
  90.8 6.0 %all_gather.3 = bf16[2,256,896]{2,1,0:T(8,128)(2,1)S(1)} all-gather(bf16[2,128,896]{2,1,0:T(8,128)(2,1)S(1)} %shard_map.116), channel_id=1, replica_groups=mesh['x'=4,'y'=4,'z'=8,'h'=2,'c'=2] {'c'}, dimensions={1}, use_global_device_ids=true | all-gather | bytes 1376256 | tf_op jit(solution)/shard_map/all_gather | solution.py:260
  96.8 0.9 copy.17
  (3 shorter events, 0.1 us)
Async XLA Ops:
  2.6 6.9 %collective-permute-start = (bf16[144,512]{1,0:T(8,128)(2,1)S(1)}, bf16[144,512]{1,0:T(8,128)(2,1)S(1)}, u32[]{:S(2)}, u32[]{:S(2)}) collective-permute-start(bf16[144,512]{1,0:T(8,128)(2,1)S(1)} %get-tuple-element.47), channel_id=1, source_target_pairs={{4,0},{8,4},{12,8},{16,12},{20,16},{24,20},{28,24},{32,28},{36,32}... | collective-permute-start | bytes 442376 | tf_op jit(solution)/shard_map/ppermute | solution.py:198
  12.6 10.4 %collective-permute-start.2 = (bf16[2,128,896]{2,1,0:T(8,128)(2,1)S(1)}, bf16[2,128,896]{2,1,0:T(8,128)(2,1)S(1)}, u32[]{:S(2)}, u32[]{:S(2)}) collective-permute-start(bf16[2,128,896]{2,1,0:T(8,128)(2,1)S(1)} %get-tuple-element.62), channel_id=1, source_target_pairs={{0,1},{1,0},{2,3},{3,2},{4,5},{5,4},{6,7},{7,6},{8,9},{9,8},{10,11... | collective-permute-start | bytes 1376264 | tf_op jit(solution)/shard_map/ppermute | solution.py:158
  23.0 10.6 %copy-start = (s32[1,2]{1,0:T(1,128)S(1)}, s32[1,2]{1,0:T(1,128)}, u32[]{:S(2)}) copy-start(s32[1,2]{1,0:T(1,128)} %documents_in.1) | copy-start | bytes 28
  23.1 67.6 %collective-permute-start.3 = (bf16[2,128,896]{2,1,0:T(8,128)(2,1)S(1)}, bf16[2,128,896]{2,1,0:T(8,128)(2,1)S(1)}, u32[]{:S(2)}, u32[]{:S(2)}) collective-permute-start(bf16[2,128,896]{2,1,0:T(8,128)(2,1)S(1)} %shard_map.115.near), channel_id=1, source_target_pairs={{0,2},{2,0},{1,3},{3,1},{4,6},{6,4},{5,7},{7,5},{8,10},{10,8},{9,1... | collective-permute-start | bytes 1376264 | tf_op jit(solution)/shard_map/ppermute | solution.py:158
  67.0 22.9 %collective-permute-start.1 = (bf16[128,512]{1,0:T(8,128)(2,1)S(1)}, bf16[128,512]{1,0:T(8,128)(2,1)S(1)}, u32[]{:S(2)}, u32[]{:S(2)}) collective-permute-start(bf16[128,512]{1,0:T(8,128)(2,1)S(1)} %get-tuple-element.56), channel_id=1, source_target_pairs={{0,4},{4,8},{8,12},{12,16},{16,20},{20,24},{24,28},{28,32},{32,36}... | collective-permute-start | bytes 393224 | tf_op jit(solution)/shard_map/ppermute | solution.py:249

commit v3 on v2

--- a/solution.py
+++ b/solution.py
@@ -60,26 +60,43 @@
     kept[...] = partial_of(core)
 
 
-def load(documents_in, ids_in, neighbours_in, key_in, value_in, queries_in, grad_in, *rest):
-    payload, documents, ids, neighbours, key_weight, value_weight, queries, grad_out, sems = rest
-    moves = (
-        (documents_in, documents),
-        (queries_in.at[0, 0:STRETCH], payload.at[0:STRETCH]),
-        (grad_in.at[0, 0:STRETCH], payload.at[STRETCH:2 * STRETCH]),
-        (neighbours_in.at[0], neighbours),
-        (key_in, key_weight),
-        (value_in, value_weight),
-        (queries_in.at[0, STRETCH:2 * STRETCH], queries),
-        (grad_in.at[0, STRETCH:2 * STRETCH], grad_out),
-        (ids_in.at[0], ids),
-    )
+def copy_all(moves, sems):
     copies = [pltpu.make_async_copy(*move, sems.at[i]) for i, move in enumerate(moves)]
     for copy in copies:
         copy.start()
+    return copies
+
+
+def pack(documents_in, queries_in, grad_in, payload, documents, sems):
+    copies = copy_all(
+        (
+            (documents_in, documents),
+            (queries_in.at[0, 0:STRETCH], payload.at[0:STRETCH]),
+            (grad_in.at[0, 0:STRETCH], payload.at[STRETCH:2 * STRETCH]),
+        ),
+        sems,
+    )
     copies[0].wait()
     first = documents[0:1, 0:1].astype(F32)
     payload[2 * STRETCH:, :] = jnp.broadcast_to(first, (16, payload.shape[1])).astype(BF16)
     for copy in copies[1:]:
+        copy.wait()
+
+
+def load(ids_in, neighbours_in, key_in, value_in, queries_in, grad_in, *rest):
+    ids, neighbours, key_weight, value_weight, queries, grad_out, sems = rest
+    copies = copy_all(
+        (
+            (neighbours_in.at[0], neighbours),
+            (key_in, key_weight),
+            (value_in, value_weight),
+            (queries_in.at[0, STRETCH:2 * STRETCH], queries),
+            (grad_in.at[0, STRETCH:2 * STRETCH], grad_out),
+            (ids_in.at[0], ids),
+        ),
+        sems,
+    )
+    for copy in copies:
         copy.wait()
 
 
@@ -122,7 +139,7 @@
         weight_grad[:, side * width:(side + 1) * width] = total.astype(BF16)
 
 
-def join(weight_rows, answer, second_attended, second_queries, attended, grad_queries):
+def join(answer, second_attended, second_queries, attended, grad_queries):
     attended[0, 0:STRETCH, :] = answer[0:STRETCH, :]
     attended[0, STRETCH:, :] = second_attended[...]
     grad_queries[0, 0:STRETCH, :] = answer[STRETCH:, :]
@@ -133,7 +150,7 @@
     chip_sum[...] = (kept[...] + got[...].astype(F32)).astype(BF16)
 
 
-def finish(near, far, weight_rows, halves):
+def finish(near, far, rows, attended, halves):
     halves[...] = (near[...].astype(F32) + far[...].astype(F32)).astype(BF16)
 
 
@@ -178,11 +195,18 @@
     half = slots // 2
     run_count = lax.axis_size("y") * lax.axis_size("z")
     half_rows = [((half, enc_width), F32), ((half, enc_width), BF16)]
-    payload, documents, ids, encodings, key_local, value_local, second_queries, second_grad = call(
+    payload, documents = call(
+        pack,
+        [((2 * STRETCH + 16, width), BF16), (block_document.shape, jnp.int32)],
+        0,
+        300_000,
+        space=pltpu.HBM,
+        scratch=[pltpu.SemaphoreType.DMA((3,))],
+    )(block_document, queries, grad_out)
+    payload = lax.ppermute(payload, ("y", "z"), [(i, i - 1) for i in range(1, run_count)])
+    ids, encodings, key_local, value_local, second_queries, second_grad = call(
         load,
         [
-            ((2 * STRETCH + 16, width), BF16),
-            (block_document.shape, jnp.int32),
             (neighbour_ids.shape[1:], jnp.int32),
             (neighbours.shape[1:], BF16),
             (key_weight.shape, BF16),
@@ -193,9 +217,8 @@
         0,
         6_000_000,
         space=pltpu.HBM,
-        scratch=[pltpu.SemaphoreType.DMA((9,))],
-    )(block_document, neighbour_ids, neighbours, key_weight, value_weight, queries, grad_out)
-    payload = lax.ppermute(payload, ("y", "z"), [(i, i - 1) for i in range(1, run_count)])
+        scratch=[pltpu.SemaphoreType.DMA((6,))],
+    )(neighbour_ids, neighbours, key_weight, value_weight, queries, grad_out)
 
     attended, grad_queries, keys_a, values_a, kept_a, sent_a, next_keys, next_values = call(
         own_pair,
@@ -234,10 +257,6 @@
         rows = rows.reshape(depth, -1, 2 * width)
         return jnp.pad(rows, ((0, 0), (0, 8 - rows.shape[1]), (0, 0))).astype(BF16)
 
-    def sum_over_depth(rows):
-        rows = lax.all_to_all(rows, "z", 0, 0, tiled=True)
-        return jnp.sum(rows.astype(F32), axis=0)
-
     always = block_document[0, 0] >= 0
     rows = lax.cond(
         always,
@@ -247,17 +266,17 @@
     )
     answer, rows = lax.optimization_barrier((answer, rows))
     answer = lax.ppermute(answer, ("y", "z"), [(i - 1, i) for i in range(1, run_count)])
-    weight_rows = lax.cond(
-        always, sum_over_depth, lambda rows: jnp.zeros(rows.shape[1:], F32), rows
-    )
+    weight_rows = lax.all_to_all(rows, "z", 0, 0, tiled=True)
     attended, grad_queries = call(join, [((1, tokens, width), BF16)] * 2, 1_000_000, 1_000_000)(
-        weight_rows, answer, attended, grad_queries
-    )
-
-    (halves,) = call(finish, [((2, half, enc_width), BF16)], 1_000_000, 1_000_000)(
-        chip_sum, far_sum, weight_rows
+        answer, attended, grad_queries
+    )
+
+    (halves,) = call(finish, [((2, half, enc_width), BF16)], 200_000_000_000, 1_000_000)(
+        chip_sum, far_sum, rows, attended
     )
     grad_rows = lax.all_gather(halves, "c", axis=1, tiled=True)
+    weight_rows, grad_rows = lax.optimization_barrier((weight_rows, grad_rows))
+    weight_rows = jnp.sum(weight_rows.astype(F32), axis=0)
     weight_rows = weight_rows[:enc_width // groups // depth]
     return (
         attended,

time: 98 us -> 95 us (0.969)
  the two profiles are of different devices: /device:TPU:1 before, /device:TPU:8 now
where the time goes in v3:
time: 95 us; the launch traced here: 94.5 us
  starting transfers between devices  35.6 us (37%)
  blocking collectives  33.6 us (35%)
  Pallas kernels  13 us (14%)
  waiting for transfers between devices  7.07 us (7%)
  local copies, waits for them, and re-layouts  3.18 us (3%)
  other arithmetic  1.27 us (1%)
    all_to_all x1, blocking collectives, sum_over_rows(): terms = lax.all_to_all(partial, ('x', 'y'), 0, 0, tiled=True)  31.2 us
    ppermute x1, starting transfers between devices, shards(): lax.ppermute(payload, ('y', 'z'), [(i, i - 1) for i in range(1, run_count)])  13 us
    pallas_call x8, Pallas kernels, run(): pl.pallas_call(kernel, out_shape=[jax.ShapeDtypeStruct(s, d) for s, d in...  13 us
    all_to_all x1, starting transfers between devices, shards(): weight_rows = lax.all_to_all(rows, 'z', 0, 0, tiled=True)  10.5 us
    ppermute x2, starting transfers between devices, swap(): return lax.ppermute(block, axis, [(0, 1), (1, 0)])  10.1 us
    all_to_all x1, waiting for transfers between devices, shards(): weight_rows = lax.all_to_all(rows, 'z', 0, 0, tiled=True)  4.42 us
    all_gather x1, blocking collectives, shards(): grad_rows = lax.all_gather(halves, 'c', axis=1, tiled=True)  2.46 us
    ppermute x1, waiting for transfers between devices, shards(): lax.ppermute(answer, ('y', 'z'), [(i - 1, i) for i in range(1, run_count)])  2.01 us
  transfers between devices with their start and end apart: 5, of which 3 were waited for; matrix products, arithmetic and copies ran while one was open for 1% of the time, Pallas kernels for 9%

profile of v3, /device:TPU:8, one launch (start us, length us, event | category | flops | bytes accessed | tf_op | source)
XLA Modules:
  0.0 94.5 jit_solution(1603209945986573788)
XLA Ops:
  0.6 0.9 shard_map.110
  1.6 13.0 %collective-permute-start = (bf16[144,512]{1,0:T(8,128)(2,1)S(1)}, bf16[144,512]{1,0:T(8,128)(2,1)S(1)}, u32[]{:S(2)}, u32[]{:S(2)}) collective-permute-start(bf16[144,512]{1,0:T(8,128)(2,1)S(1)} %get-tuple-element.45), channel_id=1, source_target_pairs={{4,0},{8,4},{12,8},{16,12},{20,16},{24,20},{28,24},{32,28},{36,32}... | collective-permute-start | bytes 442376 | tf_op jit(solution)/shard_map/ppermute | solution.py:206
  14.6 1.8 %shard_map.111 = (s32[2,256]{1,0:T(2,128)S(1)}, bf16[2,256,896]{2,1,0:T(8,128)(2,1)S(1)}, bf16[896,512]{1,0:T(8,128)(2,1)S(1)}, bf16[896,512]{1,0:T(8,128)(2,1)S...) custom-call(s32[1,2,256]{2,1,0:T(2,128)} %ids_in.1, bf16[1,2,256,896]{3,2,1,0:T(8,128)(2,1)} %neighbours_in.1, ...), custom_call_target="tpu_custom_call" | custom-call | bytes 6000000 | tf_op jit(solution)/shard_map/pallas_call | solution.py:161
  16.4 4.1 %shard_map.112 = (bf16[64,512]{1,0:T(8,128)(2,1)S(1)}, bf16[64,512]{1,0:T(8,128)(2,1)S(1)}, bf16[256,512]{1,0:T(8,128)(2,1)S(1)}, bf16[256,512]{1,0:T(8,128)(2,1...) custom-call(s32[1,2]{1,0:T(1,128)S(1)} %get-tuple-element.36.documen, ...), custom_call_target="tpu_custom_call" | custom-call | flops 1100000000 | bytes 10000000 | tf_op jit(solution)/shard_map/pallas_call | solution.py:161
  20.5 0.0 collective-permute-done.payload
  20.6 3.2 %shard_map.113 = (bf16[128,512]{1,0:T(8,128)(2,1)S(1)}, bf16[256,512]{1,0:T(8,128)(2,1)S(1)}, bf16[256,512]{1,0:T(8,128)(2,1)S(1)}, f32[2,128,896]{2,1,0:T(8,128)S(1)}, bf16[2,128,896]{2,1,0:T(8,128)(2,1)S(1)}) custom-call(s32[1,2]{1,0:T(1,128)S(1)} %get-tuple-element.36.documents, s32[2,256]{1,0:T(2,128)S(1)} %get-tuple-element.37.ids, ...), custom_call_target="tpu_custom_call" | custom-call | flops 1100000000 | bytes 10000000 | tf_op jit(solution)/shard_map/pallas_call | solution.py:161
  23.7 1.9 %collective-permute-start.2 = (bf16[2,128,896]{2,1,0:T(8,128)(2,1)S(1)}, bf16[2,128,896]{2,1,0:T(8,128)(2,1)S(1)}, u32[]{:S(2)}, u32[]{:S(2)}) collective-permute-start(bf16[2,128,896]{2,1,0:T(8,128)(2,1)S(1)} %get-tuple-element.60), channel_id=1, source_target_pairs={{0,1},{1,0},{2,3},{3,2},{4,5},{5,4},{6,7},{7,6},{8,9},{9,8},{10,11... | collective-permute-start | bytes 1376264 | tf_op jit(solution)/shard_map/ppermute | solution.py:175
  25.7 1.1 %shard_map.114.weight_grad = bf16[896,1024]{1,0:T(8,128)(2,1)S(1)} custom-call(bf16[2,256,896]{2,1,0:T(8,128)(2,1)S(1)} %get-tuple-element.40.neighbours, bf16[256,512]{1,0:T(8,128)(2,1)S(1)} %get-tuple-element.49.keys_a, bf16[256,512]{1,0:T(8,128)(2,1)S(1)} %get-tuple-element.50.keys_b, bf16[256,512]{1,0:T(8,128)(2,1)S(1)} %get-tuple-element.51.values_a, ...), custom_call_target="tpu_custom_call" | custom-call | flops 940000000 | bytes 6000000 | tf_op jit(solution)/shard_map/pallas_call | solution.py:161
  26.8 0.6 collective-permute-done.2.got
  27.5 0.0 copy-start.1
  27.5 0.1 shard_map.116.near
  27.5 8.2 %collective-permute-start.3 = (bf16[2,128,896]{2,1,0:T(8,128)(2,1)S(1)}, bf16[2,128,896]{2,1,0:T(8,128)(2,1)S(1)}, u32[]{:S(2)}, u32[]{:S(2)}) collective-permute-start(bf16[2,128,896]{2,1,0:T(8,128)(2,1)S(1)} %shard_map.116.near), channel_id=1, source_target_pairs={{0,2},{2,0},{1,3},{3,1},{4,6},{6,4},{5,7},{7,5},{8,10},{10,8},{9,1... | collective-permute-start | bytes 1376264 | tf_op jit(solution)/shard_map/ppermute | solution.py:175
  35.8 0.0 copy-done.1
  35.8 32.3 %conditional.1 = (bf16[8,8,1024]{2,1,0:T(8,128)(2,1)}) conditional(s32[]{:T(128)} %bitcast.1, () %tuple.16, bf16[896,1024]{1,0:T(8,128)(2,1)S(1)} %shard_map.114.weight_grad), branch_computations={%region_0.0_spmd, %region_1.3_spmd} | conditional | flops 860160 | bytes 6094860 | solution.py:261
  35.8 31.2 %all_to_all.12 = bf16[16,56,1024]{2,1,0:T(8,128)(2,1)S(1)} all-to-all(bf16[16,56,1024]{2,1,0:T(8,128)(2,1)S(1)} %bitcast.4), channel_id=1, replica_groups=mesh['x'=4,'y'=4,'z'=8,'h'=2,'c'=2] {'x','y'}, dimensions={0} | all-to-all | bytes 3670016 | tf_op jit(solution)/shard_map/cond/branch_1_fun/all_to_all | solution.py:255
  67.0 0.3 reduce
  67.4 0.7 pad.4
  68.1 1.9 %collective-permute-start.1 = (bf16[128,512]{1,0:T(8,128)(2,1)S(1)}, bf16[128,512]{1,0:T(8,128)(2,1)S(1)}, u32[]{:S(2)}, u32[]{:S(2)}) collective-permute-start(bf16[128,512]{1,0:T(8,128)(2,1)S(1)} %get-tuple-element.53), channel_id=1, source_target_pairs={{0,4},{4,8},{8,12},{12,16},{16,20},{20,24},{24,28},{28,32},{32,36}... | collective-permute-start | bytes 393224 | tf_op jit(solution)/shard_map/ppermute | solution.py:268
  70.0 10.5 %all-to-all-start.1 = ((bf16[8,8,1024]{2,1,0:T(8,128)(2,1)}), bf16[8,8,1024]{2,1,0:T(8,128)(2,1)}, u32[]{:S(2)}, u32[]{:S(2)}) async-start(bf16[8,8,1024]{2,1,0:T(8,128)(2,1)} %get-tuple-element.75.rows), calls=%async_computation.1 | async-start | bytes 262144 | tf_op jit(solution)/shard_map/all_to_all | solution.py:269
  80.5 2.0 %collective-permute-done.1.answer = bf16[128,512]{1,0:T(8,128)(2,1)S(1)} collective-permute-done((bf16[128,512]{1,0:T(8,128)(2,1)S(1)}, bf16[128,512]{1,0:T(8,128)(2,1)S(1)}, u32[]{:S(2)}, u32[]{:S(2)}) %collective-permute-start.1) | collective-permute-done | bytes 131104 | tf_op jit(solution)/shard_map/ppermute | solution.py:268
  82.5 0.7 shard_map.115
  83.3 0.0 collective-permute-done.3.far
  83.3 0.0 copy-start
  83.3 0.9 copy-done
  84.2 1.0 %shard_map.117 = bf16[2,128,896]{2,1,0:T(8,128)(2,1)S(1)} custom-call(bf16[2,128,896]{2,1,0:T(8,128)(2,1)S(1)} %shard_map.116.near, bf16[2,128,896]{2,1,0:T(8,128)(2,1)S(1)} %collective-permute-done.3.far, bf16[8,8,1024]{2,1,0:T(8,128)(2,1)} %get-tuple-element.75.rows, bf16[1,128,512]{2,1,0:T(8,128)(2,1)S(1)} %copy-done), custom_call_target="tpu_custom_call" | custom-call | flops 199999995904 | bytes 1000000 | tf_op jit(solution)/shard_map/pallas_call | solution.py:161
  85.2 2.5 %all_gather.3 = bf16[2,256,896]{2,1,0:T(8,128)(2,1)S(1)} all-gather(bf16[2,128,896]{2,1,0:T(8,128)(2,1)S(1)} %shard_map.117), channel_id=1, replica_groups=mesh['x'=4,'y'=4,'z'=8,'h'=2,'c'=2] {'c'}, dimensions={1}, use_global_device_ids=true | all-gather | bytes 1376256 | tf_op jit(solution)/shard_map/all_gather | solution.py:277
  87.6 4.4 %all-to-all-done.1 = bf16[8,8,1024]{2,1,0:T(8,128)(2,1)} async-done(((bf16[8,8,1024]{2,1,0:T(8,128)(2,1)}), bf16[8,8,1024]{2,1,0:T(8,128)(2,1)}, u32[]{:S(2)}, u32[]{:S(2)}) %all-to-all-start.1) | async-done | bytes 131104 | tf_op jit(solution)/shard_map/all_to_all | solution.py:269
  92.1 0.9 convert_reduce_fusion
  93.0 0.6 fusion
  93.6 0.9 copy.15
  (1 shorter events, 0.0 us)
Async XLA Ops:
  1.6 19.0 %collective-permute-start = (bf16[144,512]{1,0:T(8,128)(2,1)S(1)}, bf16[144,512]{1,0:T(8,128)(2,1)S(1)}, u32[]{:S(2)}, u32[]{:S(2)}) collective-permute-start(bf16[144,512]{1,0:T(8,128)(2,1)S(1)} %get-tuple-element.45), channel_id=1, source_target_pairs={{4,0},{8,4},{12,8},{16,12},{20,16},{24,20},{28,24},{32,28},{36,32}... | collective-permute-start | bytes 442376 | tf_op jit(solution)/shard_map/ppermute | solution.py:206
  23.7 3.7 %collective-permute-start.2 = (bf16[2,128,896]{2,1,0:T(8,128)(2,1)S(1)}, bf16[2,128,896]{2,1,0:T(8,128)(2,1)S(1)}, u32[]{:S(2)}, u32[]{:S(2)}) collective-permute-start(bf16[2,128,896]{2,1,0:T(8,128)(2,1)S(1)} %get-tuple-element.60), channel_id=1, source_target_pairs={{0,1},{1,0},{2,3},{3,2},{4,5},{5,4},{6,7},{7,6},{8,9},{9,8},{10,11... | collective-permute-start | bytes 1376264 | tf_op jit(solution)/shard_map/ppermute | solution.py:175
  27.5 8.3 %copy-start.1 = (s32[1,2]{1,0:T(1,128)S(1)}, s32[1,2]{1,0:T(1,128)}, u32[]{:S(2)}) copy-start(s32[1,2]{1,0:T(1,128)} %documents_in.1) | copy-start | bytes 28
  27.5 55.7 %collective-permute-start.3 = (bf16[2,128,896]{2,1,0:T(8,128)(2,1)S(1)}, bf16[2,128,896]{2,1,0:T(8,128)(2,1)S(1)}, u32[]{:S(2)}, u32[]{:S(2)}) collective-permute-start(bf16[2,128,896]{2,1,0:T(8,128)(2,1)S(1)} %shard_map.116.near), channel_id=1, source_target_pairs={{0,2},{2,0},{1,3},{3,1},{4,6},{6,4},{5,7},{7,5},{8,10},{10,8},{9,1... | collective-permute-start | bytes 1376264 | tf_op jit(solution)/shard_map/ppermute | solution.py:175
  68.1 14.5 %collective-permute-start.1 = (bf16[128,512]{1,0:T(8,128)(2,1)S(1)}, bf16[128,512]{1,0:T(8,128)(2,1)S(1)}, u32[]{:S(2)}, u32[]{:S(2)}) collective-permute-start(bf16[128,512]{1,0:T(8,128)(2,1)S(1)} %get-tuple-element.53), channel_id=1, source_target_pairs={{0,4},{4,8},{8,12},{12,16},{16,20},{20,24},{24,28},{28,32},{32,36}... | collective-permute-start | bytes 393224 | tf_op jit(solution)/shard_map/ppermute | solution.py:268
  70.0 22.1 %all-to-all-start.1 = ((bf16[8,8,1024]{2,1,0:T(8,128)(2,1)}), bf16[8,8,1024]{2,1,0:T(8,128)(2,1)}, u32[]{:S(2)}, u32[]{:S(2)}) async-start(bf16[8,8,1024]{2,1,0:T(8,128)(2,1)} %get-tuple-element.75.rows), calls=%async_computation.1 | async-start | bytes 262144 | tf_op jit(solution)/shard_map/all_to_all | solution.py:269
  83.3 0.9 copy-start

commit v4 on v3

--- a/solution.py
+++ b/solution.py
@@ -139,19 +139,27 @@
         weight_grad[:, side * width:(side + 1) * width] = total.astype(BF16)
 
 
-def join(answer, second_attended, second_queries, attended, grad_queries):
+def add_cores(kept, got, weight_grad, chip_sum):
+    chip_sum[...] = (kept[...] + got[...].astype(F32)).astype(BF16)
+
+
+def finish(near, far, rows, answer, second_attended, second_queries, *out):
+    halves, attended, grad_queries = out
+    halves[...] = (near[...].astype(F32) + far[...].astype(F32)).astype(BF16)
     attended[0, 0:STRETCH, :] = answer[0:STRETCH, :]
     attended[0, STRETCH:, :] = second_attended[...]
     grad_queries[0, 0:STRETCH, :] = answer[STRETCH:, :]
     grad_queries[0, STRETCH:, :] = second_queries[...]
 
 
-def add_cores(kept, got, weight_grad, chip_sum):
-    chip_sum[...] = (kept[...] + got[...].astype(F32)).astype(BF16)
-
-
-def finish(near, far, rows, attended, halves):
-    halves[...] = (near[...].astype(F32) + far[...].astype(F32)).astype(BF16)
+def sum_depth(terms, rows_in, key_grad, value_grad, rows_out):
+    rows_out[0] = rows_in[...]
+    total = terms[0].astype(F32)
+    for part in range(1, terms.shape[0]):
+        total += terms[part].astype(F32)
+    own, width = key_grad.shape
+    key_grad[...] = total[0:own, 0:width]
+    value_grad[...] = total[0:own, width:]
 
 
 def call(kernel, out_shapes, flops, moved, space=pltpu.VMEM, scratch=()):
@@ -267,24 +275,20 @@
     answer, rows = lax.optimization_barrier((answer, rows))
     answer = lax.ppermute(answer, ("y", "z"), [(i - 1, i) for i in range(1, run_count)])
     weight_rows = lax.all_to_all(rows, "z", 0, 0, tiled=True)
-    attended, grad_queries = call(join, [((1, tokens, width), BF16)] * 2, 1_000_000, 1_000_000)(
-        answer, attended, grad_queries
-    )
-
-    (halves,) = call(finish, [((2, half, enc_width), BF16)], 200_000_000_000, 1_000_000)(
-        chip_sum, far_sum, rows, attended
-    )
+    halves, attended, grad_queries = call(
+        finish,
+        [((2, half, enc_width), BF16)] + [((1, tokens, width), BF16)] * 2,
+        200_000_000_000,
+        1_000_000,
+    )(chip_sum, far_sum, rows, answer, attended, grad_queries)
     grad_rows = lax.all_gather(halves, "c", axis=1, tiled=True)
-    weight_rows, grad_rows = lax.optimization_barrier((weight_rows, grad_rows))
-    weight_rows = jnp.sum(weight_rows.astype(F32), axis=0)
-    weight_rows = weight_rows[:enc_width // groups // depth]
-    return (
-        attended,
-        grad_queries,
-        grad_rows[None],
-        weight_rows[:, :width],
-        weight_rows[:, width:],
-    )
+    key_grad, value_grad, grad_rows = call(
+        sum_depth,
+        [((enc_width // groups // depth, width), F32)] * 2 + [(neighbours.shape, BF16)],
+        1_000_000,
+        2_000_000,
+    )(weight_rows, grad_rows)
+    return attended, grad_queries, grad_rows, key_grad, value_grad
 
 
 def solution(mesh):

time: 95 us -> 94.4 us (level)
  local copies, waits for them, and re-layouts: 3.18 us -> 0.73 us
  Pallas kernels: 13 us -> 14.8 us
  waiting for transfers between devices: 7.07 us -> 8.09 us
    unnamed x5 -> x2, local copies, waits for them, and re-layouts: 1.83 us -> 0.01 us
    pallas_call x8, Pallas kernels: 13 us -> 14.8 us  [run(): pl.pallas_call(kernel, out_shape=[jax.ShapeDtypeStruct(s, d) for s, d in...]
    all_to_all x1, waiting for transfers between devices: 4.42 us -> 5.45 us  [shards(): weight_rows = lax.all_to_all(rows, 'z', 0, 0, tiled=True)]
where the time goes in v4:
time: 94.4 us; the launch traced here: 94 us
  starting transfers between devices  35.6 us (38%)
  blocking collectives  33.6 us (36%)
  Pallas kernels  14.8 us (16%)
  waiting for transfers between devices  8.09 us (9%)
    all_to_all x1, blocking collectives, sum_over_rows(): terms = lax.all_to_all(partial, ('x', 'y'), 0, 0, tiled=True)  31.2 us
    pallas_call x8, Pallas kernels, run(): pl.pallas_call(kernel, out_shape=[jax.ShapeDtypeStruct(s, d) for s, d in...  14.8 us
    ppermute x1, starting transfers between devices, shards(): lax.ppermute(payload, ('y', 'z'), [(i, i - 1) for i in range(1, run_count)])  13 us
    all_to_all x1, starting transfers between devices, shards(): weight_rows = lax.all_to_all(rows, 'z', 0, 0, tiled=True)  10.5 us
    ppermute x2, starting transfers between devices, swap(): return lax.ppermute(block, axis, [(0, 1), (1, 0)])  10.1 us
    all_to_all x1, waiting for transfers between devices, shards(): weight_rows = lax.all_to_all(rows, 'z', 0, 0, tiled=True)  5.45 us
    all_gather x1, blocking collectives, shards(): grad_rows = lax.all_gather(halves, 'c', axis=1, tiled=True)  2.45 us
    ppermute x1, waiting for transfers between devices, shards(): lax.ppermute(answer, ('y', 'z'), [(i - 1, i) for i in range(1, run_count)])  2.01 us
  transfers between devices with their start and end apart: 5, of which 3 were waited for; matrix products, arithmetic and copies ran while one was open for 1% of the time, Pallas kernels for 9%

profile of v4, /device:TPU:8, one launch (start us, length us, event | category | flops | bytes accessed | tf_op | source)
XLA Modules:
  0.0 94.0 jit_solution(16084900571223709178)
XLA Ops:
  0.6 0.9 shard_map.110
  1.6 13.0 %collective-permute-start = (bf16[144,512]{1,0:T(8,128)(2,1)S(1)}, bf16[144,512]{1,0:T(8,128)(2,1)S(1)}, u32[]{:S(2)}, u32[]{:S(2)}) collective-permute-start(bf16[144,512]{1,0:T(8,128)(2,1)S(1)} %get-tuple-element.47), channel_id=1, source_target_pairs={{4,0},{8,4},{12,8},{16,12},{20,16},{24,20},{28,24},{32,28},{36,32}... | collective-permute-start | bytes 442376 | tf_op jit(solution)/shard_map/ppermute | solution.py:214
  14.6 1.8 %shard_map.111 = (s32[2,256]{1,0:T(2,128)S(1)}, bf16[2,256,896]{2,1,0:T(8,128)(2,1)S(1)}, bf16[896,512]{1,0:T(8,128)(2,1)S(1)}, bf16[896,512]{1,0:T(8,128)(2,1)S...) custom-call(s32[1,2,256]{2,1,0:T(2,128)} %ids_in.1, bf16[1,2,256,896]{3,2,1,0:T(8,128)(2,1)} %neighbours_in.1, ...), custom_call_target="tpu_custom_call" | custom-call | bytes 6000000 | tf_op jit(solution)/shard_map/pallas_call | solution.py:169
  16.4 4.1 %shard_map.112 = (bf16[64,512]{1,0:T(8,128)(2,1)S(1)}, bf16[64,512]{1,0:T(8,128)(2,1)S(1)}, bf16[256,512]{1,0:T(8,128)(2,1)S(1)}, bf16[256,512]{1,0:T(8,128)(2,1...) custom-call(s32[1,2]{1,0:T(1,128)S(1)} %get-tuple-element.38.documen, ...), custom_call_target="tpu_custom_call" | custom-call | flops 1100000000 | bytes 10000000 | tf_op jit(solution)/shard_map/pallas_call | solution.py:169
  20.5 0.0 collective-permute-done.payload
  20.6 3.2 %shard_map.113 = (bf16[128,512]{1,0:T(8,128)(2,1)S(1)}, bf16[256,512]{1,0:T(8,128)(2,1)S(1)}, bf16[256,512]{1,0:T(8,128)(2,1)S(1)}, f32[2,128,896]{2,1,0:T(8,128)S(1)}, bf16[2,128,896]{2,1,0:T(8,128)(2,1)S(1)}) custom-call(s32[1,2]{1,0:T(1,128)S(1)} %get-tuple-element.38.documents, s32[2,256]{1,0:T(2,128)S(1)} %get-tuple-element.39.ids, ...), custom_call_target="tpu_custom_call" | custom-call | flops 1100000000 | bytes 10000000 | tf_op jit(solution)/shard_map/pallas_call | solution.py:169
  23.7 1.9 %collective-permute-start.1 = (bf16[2,128,896]{2,1,0:T(8,128)(2,1)S(1)}, bf16[2,128,896]{2,1,0:T(8,128)(2,1)S(1)}, u32[]{:S(2)}, u32[]{:S(2)}) collective-permute-start(bf16[2,128,896]{2,1,0:T(8,128)(2,1)S(1)} %get-tuple-element.51), channel_id=1, source_target_pairs={{0,1},{1,0},{2,3},{3,2},{4,5},{5,4},{6,7},{7,6},{8,9},{9,8},{10,11... | collective-permute-start | bytes 1376264 | tf_op jit(solution)/shard_map/ppermute | solution.py:183
  25.7 1.1 %shard_map.114.weight_grad = bf16[896,1024]{1,0:T(8,128)(2,1)S(1)} custom-call(bf16[2,256,896]{2,1,0:T(8,128)(2,1)S(1)} %get-tuple-element.42.neighbours, bf16[256,512]{1,0:T(8,128)(2,1)S(1)} %get-tuple-element.52.keys_a, bf16[256,512]{1,0:T(8,128)(2,1)S(1)} %get-tuple-element.53.keys_b, bf16[256,512]{1,0:T(8,128)(2,1)S(1)} %get-tuple-element.54.values_a, ...), custom_call_target="tpu_custom_call" | custom-call | flops 940000000 | bytes 6000000 | tf_op jit(solution)/shard_map/pallas_call | solution.py:169
  26.8 0.6 collective-permute-done.1.got
  27.5 0.0 copy-start
  27.5 0.1 shard_map.115.near
  27.5 8.2 %collective-permute-start.2 = (bf16[2,128,896]{2,1,0:T(8,128)(2,1)S(1)}, bf16[2,128,896]{2,1,0:T(8,128)(2,1)S(1)}, u32[]{:S(2)}, u32[]{:S(2)}) collective-permute-start(bf16[2,128,896]{2,1,0:T(8,128)(2,1)S(1)} %shard_map.115.near), channel_id=1, source_target_pairs={{0,2},{2,0},{1,3},{3,1},{4,6},{6,4},{5,7},{7,5},{8,10},{10,8},{9,1... | collective-permute-start | bytes 1376264 | tf_op jit(solution)/shard_map/ppermute | solution.py:183
  35.8 0.0 copy-done
  35.8 32.3 %conditional.1 = (bf16[8,8,1024]{2,1,0:T(8,128)(2,1)}) conditional(s32[]{:T(128)} %bitcast.1, () %tuple.15, bf16[896,1024]{1,0:T(8,128)(2,1)S(1)} %shard_map.114.weight_grad), branch_computations={%region_0.0_spmd, %region_1.3_spmd} | conditional | flops 860160 | bytes 6094860 | solution.py:269
  35.8 31.2 %all_to_all.12 = bf16[16,56,1024]{2,1,0:T(8,128)(2,1)S(1)} all-to-all(bf16[16,56,1024]{2,1,0:T(8,128)(2,1)S(1)} %bitcast.3), channel_id=1, replica_groups=mesh['x'=4,'y'=4,'z'=8,'h'=2,'c'=2] {'x','y'}, dimensions={0} | all-to-all | bytes 3670016 | tf_op jit(solution)/shard_map/cond/branch_1_fun/all_to_all | solution.py:263
  67.0 0.3 reduce
  67.4 0.7 pad.4
  68.1 1.9 %collective-permute-start.3 = (bf16[128,512]{1,0:T(8,128)(2,1)S(1)}, bf16[128,512]{1,0:T(8,128)(2,1)S(1)}, u32[]{:S(2)}, u32[]{:S(2)}) collective-permute-start(bf16[128,512]{1,0:T(8,128)(2,1)S(1)} %get-tuple-element.58), channel_id=1, source_target_pairs={{0,4},{4,8},{8,12},{12,16},{16,20},{20,24},{24,28},{28,32},{32,36}... | collective-permute-start | bytes 393224 | tf_op jit(solution)/shard_map/ppermute | solution.py:276
  70.0 10.5 %all-to-all-start.1 = ((bf16[8,8,1024]{2,1,0:T(8,128)(2,1)}), bf16[8,8,1024]{2,1,0:T(8,128)(2,1)}, u32[]{:S(2)}, u32[]{:S(2)}) async-start(bf16[8,8,1024]{2,1,0:T(8,128)(2,1)} %get-tuple-element.67.rows), calls=%async_computation.1 | async-start | bytes 262144 | tf_op jit(solution)/shard_map/all_to_all | solution.py:277
  80.5 2.0 %collective-permute-done.3.answer = bf16[128,512]{1,0:T(8,128)(2,1)S(1)} collective-permute-done((bf16[128,512]{1,0:T(8,128)(2,1)S(1)}, bf16[128,512]{1,0:T(8,128)(2,1)S(1)}, u32[]{:S(2)}, u32[]{:S(2)}) %collective-permute-start.3) | collective-permute-done | bytes 131104 | tf_op jit(solution)/shard_map/ppermute | solution.py:276
  82.5 0.0 collective-permute-done.2.far
  82.5 1.6 %shard_map.116 = (bf16[2,128,896]{2,1,0:T(8,128)(2,1)S(1)}, bf16[1,128,512]{2,1,0:T(8,128)(2,1)}, bf16[1,128,512]{2,1,0:T(8,128)(2,1)}) custom-call(bf16[2,128,896]{2,1,0:T(8,128)(2,1)S(1)} %shard_map.115.near, bf16[2,128,896]{2,1,0:T(8,128)(2,1)S(1)} %collective-permute-done.2.far, bf16[8,8,1024]{2,1,0:T(8,128)(2,1)} %get-tuple-element.67.rows, ...), custom_call_target="tpu_custom_call" | custom-call | flops 199999995904 | bytes 1000000 | tf_op jit(solution)/shard_map/pallas_call | solution.py:169
  84.2 2.4 %all_gather.3.rows_in = bf16[2,256,896]{2,1,0:T(8,128)(2,1)S(1)} all-gather(bf16[2,128,896]{2,1,0:T(8,128)(2,1)S(1)} %get-tuple-element.63), channel_id=1, replica_groups=mesh['x'=4,'y'=4,'z'=8,'h'=2,'c'=2] {'c'}, dimensions={1}, use_global_device_ids=true | all-gather | bytes 1376256 | tf_op jit(solution)/shard_map/all_gather | solution.py:284
  86.6 5.4 %all-to-all-done.1.terms = bf16[8,8,1024]{2,1,0:T(8,128)(2,1)} async-done(((bf16[8,8,1024]{2,1,0:T(8,128)(2,1)}), bf16[8,8,1024]{2,1,0:T(8,128)(2,1)}, u32[]{:S(2)}, u32[]{:S(2)}) %all-to-all-start.1) | async-done | bytes 131104 | tf_op jit(solution)/shard_map/all_to_all | solution.py:277
  92.1 1.9 %shard_map.117 = (f32[7,512]{1,0:T(8,128)}, f32[7,512]{1,0:T(8,128)}, bf16[1,2,256,896]{3,2,1,0:T(8,128)(2,1)}) custom-call(bf16[8,8,1024]{2,1,0:T(8,128)(2,1)} %all-to-all-done.1.terms, bf16[2,256,896]{2,1,0:T(8,128)(2,1)S(1)} %all_gather.3.rows_in), custom_call_target="tpu_custom_call" | custom-call | flops 1000000 | bytes 2000000 | tf_op jit(solution)/shard_map/pallas_call | solution.py:169
  (1 shorter events, 0.0 us)
Async XLA Ops:
  1.6 19.0 %collective-permute-start = (bf16[144,512]{1,0:T(8,128)(2,1)S(1)}, bf16[144,512]{1,0:T(8,128)(2,1)S(1)}, u32[]{:S(2)}, u32[]{:S(2)}) collective-permute-start(bf16[144,512]{1,0:T(8,128)(2,1)S(1)} %get-tuple-element.47), channel_id=1, source_target_pairs={{4,0},{8,4},{12,8},{16,12},{20,16},{24,20},{28,24},{32,28},{36,32}... | collective-permute-start | bytes 442376 | tf_op jit(solution)/shard_map/ppermute | solution.py:214
  23.7 3.7 %collective-permute-start.1 = (bf16[2,128,896]{2,1,0:T(8,128)(2,1)S(1)}, bf16[2,128,896]{2,1,0:T(8,128)(2,1)S(1)}, u32[]{:S(2)}, u32[]{:S(2)}) collective-permute-start(bf16[2,128,896]{2,1,0:T(8,128)(2,1)S(1)} %get-tuple-element.51), channel_id=1, source_target_pairs={{0,1},{1,0},{2,3},{3,2},{4,5},{5,4},{6,7},{7,6},{8,9},{9,8},{10,11... | collective-permute-start | bytes 1376264 | tf_op jit(solution)/shard_map/ppermute | solution.py:183
  27.5 8.3 %copy-start = (s32[1,2]{1,0:T(1,128)S(1)}, s32[1,2]{1,0:T(1,128)}, u32[]{:S(2)}) copy-start(s32[1,2]{1,0:T(1,128)} %documents_in.1) | copy-start | bytes 28
  27.5 55.0 %collective-permute-start.2 = (bf16[2,128,896]{2,1,0:T(8,128)(2,1)S(1)}, bf16[2,128,896]{2,1,0:T(8,128)(2,1)S(1)}, u32[]{:S(2)}, u32[]{:S(2)}) collective-permute-start(bf16[2,128,896]{2,1,0:T(8,128)(2,1)S(1)} %shard_map.115.near), channel_id=1, source_target_pairs={{0,2},{2,0},{1,3},{3,1},{4,6},{6,4},{5,7},{7,5},{8,10},{10,8},{9,1... | collective-permute-start | bytes 1376264 | tf_op jit(solution)/shard_map/ppermute | solution.py:183
  68.1 14.5 %collective-permute-start.3 = (bf16[128,512]{1,0:T(8,128)(2,1)S(1)}, bf16[128,512]{1,0:T(8,128)(2,1)S(1)}, u32[]{:S(2)}, u32[]{:S(2)}) collective-permute-start(bf16[128,512]{1,0:T(8,128)(2,1)S(1)} %get-tuple-element.58), channel_id=1, source_target_pairs={{0,4},{4,8},{8,12},{12,16},{16,20},{20,24},{24,28},{28,32},{32,36}... | collective-permute-start | bytes 393224 | tf_op jit(solution)/shard_map/ppermute | solution.py:276
  70.0 22.1 %all-to-all-start.1 = ((bf16[8,8,1024]{2,1,0:T(8,128)(2,1)}), bf16[8,8,1024]{2,1,0:T(8,128)(2,1)}, u32[]{:S(2)}, u32[]{:S(2)}) async-start(bf16[8,8,1024]{2,1,0:T(8,128)(2,1)} %get-tuple-element.67.rows), calls=%async_computation.1 | async-start | bytes 262144 | tf_op jit(solution)/shard_map/all_to_all | solution.py:277

commit v5 on v4

--- a/solution.py
+++ b/solution.py
@@ -47,17 +47,11 @@
         grad_values[:, span] = matmul(weights_half, grad, 0, 0).astype(BF16)
 
 
-def encoding_partials(core, key_weight, value_weight, grad_keys, grad_values, kept, sent):
-    half = kept.shape[0]
-
-    def partial_of(part):
-        rows = pl.ds(pl.multiple_of(part * half, half), half)
-        return matmul(grad_keys[rows, :], key_weight[...], 1, 1) + matmul(
-            grad_values[rows, :], value_weight[...], 1, 1
-        )
-
-    sent[...] = partial_of(1 - core).astype(BF16)
-    kept[...] = partial_of(core)
+def rows_partial(part, key_weight, value_weight, grad_keys, grad_values, half):
+    rows = pl.ds(pl.multiple_of(part * half, half), half)
+    return matmul(grad_keys[rows, :], key_weight[...], 1, 1) + matmul(
+        grad_values[rows, :], value_weight[...], 1, 1
+    )
 
 
 def copy_all(moves, sems):
@@ -108,16 +102,17 @@
         ids[0:1, :] != 0, gate,
         queries[...], grad_out[...], (attended, grad_queries, grad_keys, grad_values),
     )
-    encoding_partials(lax.axis_index("c"), key_weight, value_weight, grad_keys, grad_values, kept, sent)
+    core, grads = lax.axis_index("c"), (key_weight, value_weight, grad_keys, grad_values)
+    sent[...] = rows_partial(1 - core, *grads, sent.shape[0]).astype(BF16)
+    kept[...] = rows_partial(core, *grads, kept.shape[0])
     next_keys[...] = project(neighbours[1], key_weight)
     next_values[...] = project(neighbours[1], value_weight)
 
 
 def next_pair(
-    documents, ids, key_weight, value_weight, keys, values, payload, kept_a, sent_a, *out
+    documents, ids, key_weight, value_weight, keys, values, payload, sent_a, *out
 ):
-    answer, grad_keys, grad_values, kept, sent = out
-    kept[0] = kept_a[...]
+    answer, grad_keys, grad_values, sent = out
     sent[0] = sent_a[...]
     last_run = lax.axis_size("y") * lax.axis_size("z") - 1
     run = lax.axis_index("y") * lax.axis_size("z") + lax.axis_index("z")
@@ -129,10 +124,18 @@
         payload[0:STRETCH, :], payload[STRETCH:2 * STRETCH, :],
         (answer.at[0:STRETCH], answer.at[STRETCH:2 * STRETCH], grad_keys, grad_values),
     )
-    encoding_partials(lax.axis_index("c"), key_weight, value_weight, grad_keys, grad_values, kept.at[1], sent.at[1])
-
-
-def weight_partial(neighbours, keys_a, keys_b, values_a, values_b, weight_grad):
+    other = 1 - lax.axis_index("c")
+    partial = rows_partial(other, key_weight, value_weight, grad_keys, grad_values, sent.shape[1])
+    sent[1] = partial.astype(BF16)
+
+
+def weight_partial(
+    neighbours, key_weight, value_weight, keys_a, keys_b, values_a, values_b, kept_a,
+    weight_grad, kept,
+):
+    core, half = lax.axis_index("c"), kept.shape[1]
+    kept[0] = kept_a[...]
+    kept[1] = rows_partial(core, key_weight, value_weight, keys_b, values_b, half)
     width = keys_a.shape[1]
     for side, (first, second) in enumerate(((keys_a, keys_b), (values_a, values_b))):
         total = matmul(neighbours[0], first[...], 0, 0) + matmul(neighbours[1], second[...], 0, 0)
@@ -238,21 +241,24 @@
         10_000_000,
     )(documents, ids, encodings, key_local, value_local, second_queries, second_grad)
 
-    answer, keys_b, values_b, kept, sent = call(
+    answer, keys_b, values_b, sent = call(
         next_pair,
         [((2 * STRETCH, width), BF16)]
         + [((slots, width), BF16)] * 2
-        + [((2, half, enc_width), F32), ((2, half, enc_width), BF16)],
+        + [((2, half, enc_width), BF16)],
         1_100_000_000,
         10_000_000,
     )(
-        documents, ids, key_local, value_local, next_keys, next_values, payload, kept_a, sent_a
+        documents, ids, key_local, value_local, next_keys, next_values, payload, sent_a
     )
     got = swap(sent, "c")
 
-    (weight_grad,) = call(
-        weight_partial, [((enc_width, 2 * width), BF16)], 940_000_000, 6_000_000
-    )(encodings, keys_a, keys_b, values_a, values_b)
+    weight_grad, kept = call(
+        weight_partial,
+        [((enc_width, 2 * width), BF16), ((2, half, enc_width), F32)],
+        1_180_000_000,
+        8_000_000,
+    )(encodings, key_local, value_local, keys_a, keys_b, values_a, values_b, kept_a)
     groups = lax.axis_size("x") * lax.axis_size("y")
     depth = lax.axis_size("z")
     (chip_sum,) = call(add_cores, [((2, half, enc_width), BF16)], 1_000_000, 2_000_000)(

time: 94.4 us -> 94 us (level)
  transfers between devices with their start and end apart: 5 -> 5, of which waited for: 3 -> 3; matrix products, arithmetic and copies ran while one was open for 1% -> 1% of each run, Pallas kernels for 9% -> 10%
where the time goes in v5:
time: 94 us; the launch traced here: 93.6 us
  starting transfers between devices  35.5 us (38%)
  blocking collectives  33.9 us (36%)
  Pallas kernels  14.8 us (16%)
  waiting for transfers between devices  7.59 us (8%)
    all_to_all x1, blocking collectives, sum_over_rows(): terms = lax.all_to_all(partial, ('x', 'y'), 0, 0, tiled=True)  31.4 us
    pallas_call x8, Pallas kernels, run(): pl.pallas_call(kernel, out_shape=[jax.ShapeDtypeStruct(s, d) for s, d in...  14.8 us
    ppermute x1, starting transfers between devices, shards(): lax.ppermute(payload, ('y', 'z'), [(i, i - 1) for i in range(1, run_count)])  13 us
    all_to_all x1, starting transfers between devices, shards(): weight_rows = lax.all_to_all(rows, 'z', 0, 0, tiled=True)  10.4 us
    ppermute x2, starting transfers between devices, swap(): return lax.ppermute(block, axis, [(0, 1), (1, 0)])  10.1 us
    all_to_all x1, waiting for transfers between devices, shards(): weight_rows = lax.all_to_all(rows, 'z', 0, 0, tiled=True)  5.36 us
    all_gather x1, blocking collectives, shards(): grad_rows = lax.all_gather(halves, 'c', axis=1, tiled=True)  2.45 us
    ppermute x1, waiting for transfers between devices, shards(): lax.ppermute(answer, ('y', 'z'), [(i - 1, i) for i in range(1, run_count)])  2.11 us
  transfers between devices with their start and end apart: 5, of which 3 were waited for; matrix products, arithmetic and copies ran while one was open for 1% of the time, Pallas kernels for 10%

profile of v5, /device:TPU:8, one launch (start us, length us, event | category | flops | bytes accessed | tf_op | source)
XLA Modules:
  0.0 93.6 jit_solution(7850068273141422228)
XLA Ops:
  0.6 0.9 shard_map.111
  1.6 13.0 %collective-permute-start = (bf16[144,512]{1,0:T(8,128)(2,1)S(1)}, bf16[144,512]{1,0:T(8,128)(2,1)S(1)}, u32[]{:S(2)}, u32[]{:S(2)}) collective-permute-start(bf16[144,512]{1,0:T(8,128)(2,1)S(1)} %get-tuple-element.49), channel_id=1, source_target_pairs={{4,0},{8,4},{12,8},{16,12},{20,16},{24,20},{28,24},{32,28},{36,32}... | collective-permute-start | bytes 442376 | tf_op jit(solution)/shard_map/ppermute | solution.py:217
  14.6 1.8 %shard_map.110 = (s32[2,256]{1,0:T(2,128)S(1)}, bf16[2,256,896]{2,1,0:T(8,128)(2,1)S(1)}, bf16[896,512]{1,0:T(8,128)(2,1)S(1)}, bf16[896,512]{1,0:T(8,128)(2,1)S...) custom-call(s32[1,2,256]{2,1,0:T(2,128)} %ids_in.1, bf16[1,2,256,896]{3,2,1,0:T(8,128)(2,1)} %neighbours_in.1, ...), custom_call_target="tpu_custom_call" | custom-call | bytes 6000000 | tf_op jit(solution)/shard_map/pallas_call | solution.py:172
  16.4 4.1 %shard_map.112 = (bf16[64,512]{1,0:T(8,128)(2,1)S(1)}, bf16[64,512]{1,0:T(8,128)(2,1)S(1)}, bf16[256,512]{1,0:T(8,128)(2,1)S(1)}, bf16[256,512]{1,0:T(8,128)(2,1...) custom-call(s32[1,2]{1,0:T(1,128)S(1)} %get-tuple-element.42.documen, ...), custom_call_target="tpu_custom_call" | custom-call | flops 1100000000 | bytes 10000000 | tf_op jit(solution)/shard_map/pallas_call | solution.py:172
  20.5 0.0 collective-permute-done.payload
  20.5 2.7 %shard_map.113 = (bf16[128,512]{1,0:T(8,128)(2,1)S(1)}, bf16[256,512]{1,0:T(8,128)(2,1)S(1)}, bf16[256,512]{1,0:T(8,128)(2,1)S(1)}, bf16[2,128,896]{2,1,0:T(8,128)(2,1)S(1)}) custom-call(s32[1,2]{1,0:T(1,128)S(1)} %get-tuple-element.42.documents, s32[2,256]{1,0:T(2,128)S(1)} %get-tuple-element.43.ids, bf16[896,512]{1,0:T(8,128)(2,1)S(1)} %get-tuple-element.40.key_weight, ...), custom_call_target="tpu_custom_call" | custom-call | flops 1100000000 | bytes 10000000 | tf_op jit(solution)/shard_map/pallas_call | solution.py:172
  23.3 1.9 %collective-permute-start.1 = (bf16[2,128,896]{2,1,0:T(8,128)(2,1)S(1)}, bf16[2,128,896]{2,1,0:T(8,128)(2,1)S(1)}, u32[]{:S(2)}, u32[]{:S(2)}) collective-permute-start(bf16[2,128,896]{2,1,0:T(8,128)(2,1)S(1)} %get-tuple-element.56), channel_id=1, source_target_pairs={{0,1},{1,0},{2,3},{3,2},{4,5},{5,4},{6,7},{7,6},{8,9},{9,8},{10,11... | collective-permute-start | bytes 1376264 | tf_op jit(solution)/shard_map/ppermute | solution.py:186
  25.2 1.7 %shard_map.114 = (bf16[896,1024]{1,0:T(8,128)(2,1)S(1)}, f32[2,128,896]{2,1,0:T(8,128)S(1)}) custom-call(bf16[2,256,896]{2,1,0:T(8,128)(2,1)S(1)} %get-tuple-element.39.neighbours, bf16[896,512]{1,0:T(8,128)(2,1)S(1)} %get-tuple-element.40.key_weight, bf16[896,512]{1,0:T(8,128)(2,1)S(1)} %get-tuple-element.41.value_weight, ...), custom_call_target="tpu_custom_call" | custom-call | flops 1180000000 | bytes 8000000 | tf_op jit(solution)/shard_map/pallas_call | solution.py:172
  26.9 0.1 collective-permute-done.1.got
  27.0 0.0 copy-start
  27.0 0.1 shard_map.115.near
  27.1 8.2 %collective-permute-start.2 = (bf16[2,128,896]{2,1,0:T(8,128)(2,1)S(1)}, bf16[2,128,896]{2,1,0:T(8,128)(2,1)S(1)}, u32[]{:S(2)}, u32[]{:S(2)}) collective-permute-start(bf16[2,128,896]{2,1,0:T(8,128)(2,1)S(1)} %shard_map.115.near), channel_id=1, source_target_pairs={{0,2},{2,0},{1,3},{3,1},{4,6},{6,4},{5,7},{7,5},{8,10},{10,8},{9,1... | collective-permute-start | bytes 1376264 | tf_op jit(solution)/shard_map/ppermute | solution.py:186
  35.3 0.0 copy-done
  35.3 32.5 %conditional.1 = (bf16[8,8,1024]{2,1,0:T(8,128)(2,1)}) conditional(s32[]{:T(128)} %bitcast.1, () %tuple.15, bf16[896,1024]{1,0:T(8,128)(2,1)S(1)} %get-tuple-element.57.weight_grad), branch_computations={%region_0.0_spmd, %region_1.3_spmd} | conditional | flops 860160 | bytes 6094860 | solution.py:275
  35.3 31.4 %all_to_all.12 = bf16[16,56,1024]{2,1,0:T(8,128)(2,1)S(1)} all-to-all(bf16[16,56,1024]{2,1,0:T(8,128)(2,1)S(1)} %bitcast.3), channel_id=1, replica_groups=mesh['x'=4,'y'=4,'z'=8,'h'=2,'c'=2] {'x','y'}, dimensions={0} | all-to-all | bytes 3670016 | tf_op jit(solution)/shard_map/cond/branch_1_fun/all_to_all | solution.py:269
  66.8 0.3 reduce
  67.2 0.7 pad.4
  67.9 1.9 %collective-permute-start.3 = (bf16[128,512]{1,0:T(8,128)(2,1)S(1)}, bf16[128,512]{1,0:T(8,128)(2,1)S(1)}, u32[]{:S(2)}, u32[]{:S(2)}) collective-permute-start(bf16[128,512]{1,0:T(8,128)(2,1)S(1)} %get-tuple-element.60), channel_id=1, source_target_pairs={{0,4},{4,8},{8,12},{12,16},{16,20},{20,24},{24,28},{28,32},{32,36}... | collective-permute-start | bytes 393224 | tf_op jit(solution)/shard_map/ppermute | solution.py:282
  69.8 10.4 %all-to-all-start.1 = ((bf16[8,8,1024]{2,1,0:T(8,128)(2,1)}), bf16[8,8,1024]{2,1,0:T(8,128)(2,1)}, u32[]{:S(2)}, u32[]{:S(2)}) async-start(bf16[8,8,1024]{2,1,0:T(8,128)(2,1)} %get-tuple-element.69.rows), calls=%async_computation.1 | async-start | bytes 262144 | tf_op jit(solution)/shard_map/all_to_all | solution.py:283
  80.1 2.1 %collective-permute-done.3.answer = bf16[128,512]{1,0:T(8,128)(2,1)S(1)} collective-permute-done((bf16[128,512]{1,0:T(8,128)(2,1)S(1)}, bf16[128,512]{1,0:T(8,128)(2,1)S(1)}, u32[]{:S(2)}, u32[]{:S(2)}) %collective-permute-start.3) | collective-permute-done | bytes 131104 | tf_op jit(solution)/shard_map/ppermute | solution.py:282
  82.3 0.0 collective-permute-done.2.far
  82.3 1.6 %shard_map.116 = (bf16[2,128,896]{2,1,0:T(8,128)(2,1)S(1)}, bf16[1,128,512]{2,1,0:T(8,128)(2,1)}, bf16[1,128,512]{2,1,0:T(8,128)(2,1)}) custom-call(bf16[2,128,896]{2,1,0:T(8,128)(2,1)S(1)} %shard_map.115.near, bf16[2,128,896]{2,1,0:T(8,128)(2,1)S(1)} %collective-permute-done.2.far, bf16[8,8,1024]{2,1,0:T(8,128)(2,1)} %get-tuple-element.69.rows, ...), custom_call_target="tpu_custom_call" | custom-call | flops 199999995904 | bytes 1000000 | tf_op jit(solution)/shard_map/pallas_call | solution.py:172
  83.9 2.4 %all_gather.3.rows_in = bf16[2,256,896]{2,1,0:T(8,128)(2,1)S(1)} all-gather(bf16[2,128,896]{2,1,0:T(8,128)(2,1)S(1)} %get-tuple-element.65), channel_id=1, replica_groups=mesh['x'=4,'y'=4,'z'=8,'h'=2,'c'=2] {'c'}, dimensions={1}, use_global_device_ids=true | all-gather | bytes 1376256 | tf_op jit(solution)/shard_map/all_gather | solution.py:290
  86.3 5.4 %all-to-all-done.1.terms = bf16[8,8,1024]{2,1,0:T(8,128)(2,1)} async-done(((bf16[8,8,1024]{2,1,0:T(8,128)(2,1)}), bf16[8,8,1024]{2,1,0:T(8,128)(2,1)}, u32[]{:S(2)}, u32[]{:S(2)}) %all-to-all-start.1) | async-done | bytes 131104 | tf_op jit(solution)/shard_map/all_to_all | solution.py:283
  91.7 1.9 %shard_map.117 = (f32[7,512]{1,0:T(8,128)}, f32[7,512]{1,0:T(8,128)}, bf16[1,2,256,896]{3,2,1,0:T(8,128)(2,1)}) custom-call(bf16[8,8,1024]{2,1,0:T(8,128)(2,1)} %all-to-all-done.1.terms, bf16[2,256,896]{2,1,0:T(8,128)(2,1)S(1)} %all_gather.3.rows_in), custom_call_target="tpu_custom_call" | custom-call | flops 1000000 | bytes 2000000 | tf_op jit(solution)/shard_map/pallas_call | solution.py:172
  (1 shorter events, 0.0 us)
Async XLA Ops:
  1.6 19.0 %collective-permute-start = (bf16[144,512]{1,0:T(8,128)(2,1)S(1)}, bf16[144,512]{1,0:T(8,128)(2,1)S(1)}, u32[]{:S(2)}, u32[]{:S(2)}) collective-permute-start(bf16[144,512]{1,0:T(8,128)(2,1)S(1)} %get-tuple-element.49), channel_id=1, source_target_pairs={{4,0},{8,4},{12,8},{16,12},{20,16},{24,20},{28,24},{32,28},{36,32}... | collective-permute-start | bytes 442376 | tf_op jit(solution)/shard_map/ppermute | solution.py:217
  23.3 3.7 %collective-permute-start.1 = (bf16[2,128,896]{2,1,0:T(8,128)(2,1)S(1)}, bf16[2,128,896]{2,1,0:T(8,128)(2,1)S(1)}, u32[]{:S(2)}, u32[]{:S(2)}) collective-permute-start(bf16[2,128,896]{2,1,0:T(8,128)(2,1)S(1)} %get-tuple-element.56), channel_id=1, source_target_pairs={{0,1},{1,0},{2,3},{3,2},{4,5},{5,4},{6,7},{7,6},{8,9},{9,8},{10,11... | collective-permute-start | bytes 1376264 | tf_op jit(solution)/shard_map/ppermute | solution.py:186
  27.0 8.3 %copy-start = (s32[1,2]{1,0:T(1,128)S(1)}, s32[1,2]{1,0:T(1,128)}, u32[]{:S(2)}) copy-start(s32[1,2]{1,0:T(1,128)} %documents_in.1) | copy-start | bytes 28
  27.1 55.2 %collective-permute-start.2 = (bf16[2,128,896]{2,1,0:T(8,128)(2,1)S(1)}, bf16[2,128,896]{2,1,0:T(8,128)(2,1)S(1)}, u32[]{:S(2)}, u32[]{:S(2)}) collective-permute-start(bf16[2,128,896]{2,1,0:T(8,128)(2,1)S(1)} %shard_map.115.near), channel_id=1, source_target_pairs={{0,2},{2,0},{1,3},{3,1},{4,6},{6,4},{5,7},{7,5},{8,10},{10,8},{9,1... | collective-permute-start | bytes 1376264 | tf_op jit(solution)/shard_map/ppermute | solution.py:186
  67.9 14.4 %collective-permute-start.3 = (bf16[128,512]{1,0:T(8,128)(2,1)S(1)}, bf16[128,512]{1,0:T(8,128)(2,1)S(1)}, u32[]{:S(2)}, u32[]{:S(2)}) collective-permute-start(bf16[128,512]{1,0:T(8,128)(2,1)S(1)} %get-tuple-element.60), channel_id=1, source_target_pairs={{0,4},{4,8},{8,12},{12,16},{16,20},{20,24},{24,28},{28,32},{32,36}... | collective-permute-start | bytes 393224 | tf_op jit(solution)/shard_map/ppermute | solution.py:282
  69.8 21.9 %all-to-all-start.1 = ((bf16[8,8,1024]{2,1,0:T(8,128)(2,1)}), bf16[8,8,1024]{2,1,0:T(8,128)(2,1)}, u32[]{:S(2)}, u32[]{:S(2)}) async-start(bf16[8,8,1024]{2,1,0:T(8,128)(2,1)} %get-tuple-element.69.rows), calls=%async_computation.1 | async-start | bytes 262144 | tf_op jit(solution)/shard_map/all_to_all | solution.py:283

commit v6 on v5

--- a/solution.py
+++ b/solution.py
@@ -155,17 +155,19 @@
     grad_queries[0, STRETCH:, :] = second_queries[...]
 
 
-def sum_depth(terms, rows_in, key_grad, value_grad, rows_out):
-    rows_out[0] = rows_in[...]
+def sum_depth(terms, rows_in, key_grad, value_grad, rows_out, sem):
+    written = pltpu.make_async_copy(rows_in, rows_out.at[0], sem)
+    written.start()
     total = terms[0].astype(F32)
     for part in range(1, terms.shape[0]):
         total += terms[part].astype(F32)
     own, width = key_grad.shape
     key_grad[...] = total[0:own, 0:width]
     value_grad[...] = total[0:own, width:]
-
-
-def call(kernel, out_shapes, flops, moved, space=pltpu.VMEM, scratch=()):
+    written.wait()
+
+
+def call(kernel, out_shapes, flops, moved, space=pltpu.VMEM, scratch=(), in_hbm=0):
     def run(*arrays):
         if space == pltpu.HBM:
             arrays = [pltpu.with_memory_space_constraint(a, pltpu.HBM) for a in arrays]
@@ -173,7 +175,8 @@
             kernel,
             out_shape=[jax.ShapeDtypeStruct(s, d) for s, d in out_shapes],
             in_specs=[pl.BlockSpec(memory_space=space)] * len(arrays),
-            out_specs=[pl.BlockSpec(memory_space=pltpu.VMEM)] * len(out_shapes),
+            out_specs=[pl.BlockSpec(memory_space=pltpu.VMEM)] * (len(out_shapes) - in_hbm)
+            + [pl.BlockSpec(memory_space=pltpu.HBM)] * in_hbm,
             scratch_shapes=list(scratch),
             compiler_params=pltpu.CompilerParams(vmem_limit_bytes=48 * 2**20),
             cost_estimate=pl.CostEstimate(flops=flops, bytes_accessed=moved, transcendentals=0),
@@ -293,6 +296,8 @@
         [((enc_width // groups // depth, width), F32)] * 2 + [(neighbours.shape, BF16)],
         1_000_000,
         2_000_000,
+        scratch=[pltpu.SemaphoreType.DMA],
+        in_hbm=1,
     )(weight_rows, grad_rows)
     return attended, grad_queries, grad_rows, key_grad, value_grad
 

time: 94 us -> 94.6 us (level)
  no operation moved by 1% of the time
where the time goes in v6:
time: 94.6 us; the launch traced here: 94.1 us
  starting transfers between devices  35.5 us (38%)
  blocking collectives  33.9 us (36%)
  Pallas kernels  15.3 us (16%)
  waiting for transfers between devices  7.59 us (8%)
    all_to_all x1, blocking collectives, sum_over_rows(): terms = lax.all_to_all(partial, ('x', 'y'), 0, 0, tiled=True)  31.4 us
    pallas_call x8, Pallas kernels, run(): pl.pallas_call(kernel, out_shape=[jax.ShapeDtypeStruct(s, d) for s, d in...  15.3 us
    ppermute x1, starting transfers between devices, shards(): lax.ppermute(payload, ('y', 'z'), [(i, i - 1) for i in range(1, run_count)])  13 us
    all_to_all x1, starting transfers between devices, shards(): weight_rows = lax.all_to_all(rows, 'z', 0, 0, tiled=True)  10.4 us
    ppermute x2, starting transfers between devices, swap(): return lax.ppermute(block, axis, [(0, 1), (1, 0)])  10.1 us
    all_to_all x1, waiting for transfers between devices, shards(): weight_rows = lax.all_to_all(rows, 'z', 0, 0, tiled=True)  5.36 us
    all_gather x1, blocking collectives, shards(): grad_rows = lax.all_gather(halves, 'c', axis=1, tiled=True)  2.45 us
    ppermute x1, waiting for transfers between devices, shards(): lax.ppermute(answer, ('y', 'z'), [(i - 1, i) for i in range(1, run_count)])  2.11 us
  transfers between devices with their start and end apart: 5, of which 3 were waited for; matrix products, arithmetic and copies ran while one was open for 1% of the time, Pallas kernels for 10%

profile of v6, /device:TPU:8, one launch (start us, length us, event | category | flops | bytes accessed | tf_op | source)
XLA Modules:
  0.0 94.1 jit_solution(11249113390197862245)
XLA Ops:
  0.6 0.9 shard_map.111
  1.6 13.0 %collective-permute-start = (bf16[144,512]{1,0:T(8,128)(2,1)S(1)}, bf16[144,512]{1,0:T(8,128)(2,1)S(1)}, u32[]{:S(2)}, u32[]{:S(2)}) collective-permute-start(bf16[144,512]{1,0:T(8,128)(2,1)S(1)} %get-tuple-element.49), channel_id=1, source_target_pairs={{4,0},{8,4},{12,8},{16,12},{20,16},{24,20},{28,24},{32,28},{36,32}... | collective-permute-start | bytes 442376 | tf_op jit(solution)/shard_map/ppermute | solution.py:220
  14.6 1.8 %shard_map.110 = (s32[2,256]{1,0:T(2,128)S(1)}, bf16[2,256,896]{2,1,0:T(8,128)(2,1)S(1)}, bf16[896,512]{1,0:T(8,128)(2,1)S(1)}, bf16[896,512]{1,0:T(8,128)(2,1)S...) custom-call(s32[1,2,256]{2,1,0:T(2,128)} %ids_in.1, bf16[1,2,256,896]{3,2,1,0:T(8,128)(2,1)} %neighbours_in.1, ...), custom_call_target="tpu_custom_call" | custom-call | bytes 6000000 | tf_op jit(solution)/shard_map/pallas_call | solution.py:174
  16.4 4.1 %shard_map.112 = (bf16[64,512]{1,0:T(8,128)(2,1)S(1)}, bf16[64,512]{1,0:T(8,128)(2,1)S(1)}, bf16[256,512]{1,0:T(8,128)(2,1)S(1)}, bf16[256,512]{1,0:T(8,128)(2,1...) custom-call(s32[1,2]{1,0:T(1,128)S(1)} %get-tuple-element.42.documen, ...), custom_call_target="tpu_custom_call" | custom-call | flops 1100000000 | bytes 10000000 | tf_op jit(solution)/shard_map/pallas_call | solution.py:174
  20.5 0.0 collective-permute-done.payload
  20.5 2.7 %shard_map.113 = (bf16[128,512]{1,0:T(8,128)(2,1)S(1)}, bf16[256,512]{1,0:T(8,128)(2,1)S(1)}, bf16[256,512]{1,0:T(8,128)(2,1)S(1)}, bf16[2,128,896]{2,1,0:T(8,128)(2,1)S(1)}) custom-call(s32[1,2]{1,0:T(1,128)S(1)} %get-tuple-element.42.documents, s32[2,256]{1,0:T(2,128)S(1)} %get-tuple-element.43.ids, bf16[896,512]{1,0:T(8,128)(2,1)S(1)} %get-tuple-element.40.key_weight, ...), custom_call_target="tpu_custom_call" | custom-call | flops 1100000000 | bytes 10000000 | tf_op jit(solution)/shard_map/pallas_call | solution.py:174
  23.3 1.9 %collective-permute-start.1 = (bf16[2,128,896]{2,1,0:T(8,128)(2,1)S(1)}, bf16[2,128,896]{2,1,0:T(8,128)(2,1)S(1)}, u32[]{:S(2)}, u32[]{:S(2)}) collective-permute-start(bf16[2,128,896]{2,1,0:T(8,128)(2,1)S(1)} %get-tuple-element.56), channel_id=1, source_target_pairs={{0,1},{1,0},{2,3},{3,2},{4,5},{5,4},{6,7},{7,6},{8,9},{9,8},{10,11... | collective-permute-start | bytes 1376264 | tf_op jit(solution)/shard_map/ppermute | solution.py:189
  25.2 1.7 %shard_map.114 = (bf16[896,1024]{1,0:T(8,128)(2,1)S(1)}, f32[2,128,896]{2,1,0:T(8,128)S(1)}) custom-call(bf16[2,256,896]{2,1,0:T(8,128)(2,1)S(1)} %get-tuple-element.39.neighbours, bf16[896,512]{1,0:T(8,128)(2,1)S(1)} %get-tuple-element.40.key_weight, bf16[896,512]{1,0:T(8,128)(2,1)S(1)} %get-tuple-element.41.value_weight, ...), custom_call_target="tpu_custom_call" | custom-call | flops 1180000000 | bytes 8000000 | tf_op jit(solution)/shard_map/pallas_call | solution.py:174
  26.9 0.1 collective-permute-done.1.got
  27.0 0.0 copy-start
  27.0 0.1 shard_map.115.near
  27.1 8.2 %collective-permute-start.2 = (bf16[2,128,896]{2,1,0:T(8,128)(2,1)S(1)}, bf16[2,128,896]{2,1,0:T(8,128)(2,1)S(1)}, u32[]{:S(2)}, u32[]{:S(2)}) collective-permute-start(bf16[2,128,896]{2,1,0:T(8,128)(2,1)S(1)} %shard_map.115.near), channel_id=1, source_target_pairs={{0,2},{2,0},{1,3},{3,1},{4,6},{6,4},{5,7},{7,5},{8,10},{10,8},{9,1... | collective-permute-start | bytes 1376264 | tf_op jit(solution)/shard_map/ppermute | solution.py:189
  35.3 0.0 copy-done
  35.3 32.5 %conditional.1 = (bf16[8,8,1024]{2,1,0:T(8,128)(2,1)}) conditional(s32[]{:T(128)} %bitcast.1, () %tuple.15, bf16[896,1024]{1,0:T(8,128)(2,1)S(1)} %get-tuple-element.57.weight_grad), branch_computations={%region_0.0_spmd, %region_1.3_spmd} | conditional | flops 860160 | bytes 6094860 | solution.py:278
  35.3 31.4 %all_to_all.12 = bf16[16,56,1024]{2,1,0:T(8,128)(2,1)S(1)} all-to-all(bf16[16,56,1024]{2,1,0:T(8,128)(2,1)S(1)} %bitcast.3), channel_id=1, replica_groups=mesh['x'=4,'y'=4,'z'=8,'h'=2,'c'=2] {'x','y'}, dimensions={0} | all-to-all | bytes 3670016 | tf_op jit(solution)/shard_map/cond/branch_1_fun/all_to_all | solution.py:272
  66.8 0.3 reduce
  67.2 0.7 pad.4
  67.9 1.9 %collective-permute-start.3 = (bf16[128,512]{1,0:T(8,128)(2,1)S(1)}, bf16[128,512]{1,0:T(8,128)(2,1)S(1)}, u32[]{:S(2)}, u32[]{:S(2)}) collective-permute-start(bf16[128,512]{1,0:T(8,128)(2,1)S(1)} %get-tuple-element.60), channel_id=1, source_target_pairs={{0,4},{4,8},{8,12},{12,16},{16,20},{20,24},{24,28},{28,32},{32,36}... | collective-permute-start | bytes 393224 | tf_op jit(solution)/shard_map/ppermute | solution.py:285
  69.8 10.4 %all-to-all-start.1 = ((bf16[8,8,1024]{2,1,0:T(8,128)(2,1)}), bf16[8,8,1024]{2,1,0:T(8,128)(2,1)}, u32[]{:S(2)}, u32[]{:S(2)}) async-start(bf16[8,8,1024]{2,1,0:T(8,128)(2,1)} %get-tuple-element.69.rows), calls=%async_computation.1 | async-start | bytes 262144 | tf_op jit(solution)/shard_map/all_to_all | solution.py:286
  80.1 2.1 %collective-permute-done.3.answer = bf16[128,512]{1,0:T(8,128)(2,1)S(1)} collective-permute-done((bf16[128,512]{1,0:T(8,128)(2,1)S(1)}, bf16[128,512]{1,0:T(8,128)(2,1)S(1)}, u32[]{:S(2)}, u32[]{:S(2)}) %collective-permute-start.3) | collective-permute-done | bytes 131104 | tf_op jit(solution)/shard_map/ppermute | solution.py:285
  82.3 0.0 collective-permute-done.2.far
  82.3 1.6 %shard_map.116 = (bf16[2,128,896]{2,1,0:T(8,128)(2,1)S(1)}, bf16[1,128,512]{2,1,0:T(8,128)(2,1)}, bf16[1,128,512]{2,1,0:T(8,128)(2,1)}) custom-call(bf16[2,128,896]{2,1,0:T(8,128)(2,1)S(1)} %shard_map.115.near, bf16[2,128,896]{2,1,0:T(8,128)(2,1)S(1)} %collective-permute-done.2.far, bf16[8,8,1024]{2,1,0:T(8,128)(2,1)} %get-tuple-element.69.rows, ...), custom_call_target="tpu_custom_call" | custom-call | flops 199999995904 | bytes 1000000 | tf_op jit(solution)/shard_map/pallas_call | solution.py:174
  83.9 2.4 %all_gather.3.rows_in = bf16[2,256,896]{2,1,0:T(8,128)(2,1)S(1)} all-gather(bf16[2,128,896]{2,1,0:T(8,128)(2,1)S(1)} %get-tuple-element.65), channel_id=1, replica_groups=mesh['x'=4,'y'=4,'z'=8,'h'=2,'c'=2] {'c'}, dimensions={1}, use_global_device_ids=true | all-gather | bytes 1376256 | tf_op jit(solution)/shard_map/all_gather | solution.py:293
  86.3 5.4 %all-to-all-done.1.terms = bf16[8,8,1024]{2,1,0:T(8,128)(2,1)} async-done(((bf16[8,8,1024]{2,1,0:T(8,128)(2,1)}), bf16[8,8,1024]{2,1,0:T(8,128)(2,1)}, u32[]{:S(2)}, u32[]{:S(2)}) %all-to-all-start.1) | async-done | bytes 131104 | tf_op jit(solution)/shard_map/all_to_all | solution.py:286
  91.7 2.4 %shard_map.117 = (f32[7,512]{1,0:T(8,128)}, f32[7,512]{1,0:T(8,128)}, bf16[1,2,256,896]{3,2,1,0:T(8,128)(2,1)}) custom-call(bf16[8,8,1024]{2,1,0:T(8,128)(2,1)} %all-to-all-done.1.terms, bf16[2,256,896]{2,1,0:T(8,128)(2,1)S(1)} %all_gather.3.rows_in), custom_call_target="tpu_custom_call" | custom-call | flops 1000000 | bytes 2000000 | tf_op jit(solution)/shard_map/pallas_call | solution.py:174
  (1 shorter events, 0.0 us)
Async XLA Ops:
  1.6 19.0 %collective-permute-start = (bf16[144,512]{1,0:T(8,128)(2,1)S(1)}, bf16[144,512]{1,0:T(8,128)(2,1)S(1)}, u32[]{:S(2)}, u32[]{:S(2)}) collective-permute-start(bf16[144,512]{1,0:T(8,128)(2,1)S(1)} %get-tuple-element.49), channel_id=1, source_target_pairs={{4,0},{8,4},{12,8},{16,12},{20,16},{24,20},{28,24},{32,28},{36,32}... | collective-permute-start | bytes 442376 | tf_op jit(solution)/shard_map/ppermute | solution.py:220
  23.3 3.7 %collective-permute-start.1 = (bf16[2,128,896]{2,1,0:T(8,128)(2,1)S(1)}, bf16[2,128,896]{2,1,0:T(8,128)(2,1)S(1)}, u32[]{:S(2)}, u32[]{:S(2)}) collective-permute-start(bf16[2,128,896]{2,1,0:T(8,128)(2,1)S(1)} %get-tuple-element.56), channel_id=1, source_target_pairs={{0,1},{1,0},{2,3},{3,2},{4,5},{5,4},{6,7},{7,6},{8,9},{9,8},{10,11... | collective-permute-start | bytes 1376264 | tf_op jit(solution)/shard_map/ppermute | solution.py:189
  27.0 8.3 %copy-start = (s32[1,2]{1,0:T(1,128)S(1)}, s32[1,2]{1,0:T(1,128)}, u32[]{:S(2)}) copy-start(s32[1,2]{1,0:T(1,128)} %documents_in.1) | copy-start | bytes 28
  27.1 55.2 %collective-permute-start.2 = (bf16[2,128,896]{2,1,0:T(8,128)(2,1)S(1)}, bf16[2,128,896]{2,1,0:T(8,128)(2,1)S(1)}, u32[]{:S(2)}, u32[]{:S(2)}) collective-permute-start(bf16[2,128,896]{2,1,0:T(8,128)(2,1)S(1)} %shard_map.115.near), channel_id=1, source_target_pairs={{0,2},{2,0},{1,3},{3,1},{4,6},{6,4},{5,7},{7,5},{8,10},{10,8},{9,1... | collective-permute-start | bytes 1376264 | tf_op jit(solution)/shard_map/ppermute | solution.py:189
  67.9 14.4 %collective-permute-start.3 = (bf16[128,512]{1,0:T(8,128)(2,1)S(1)}, bf16[128,512]{1,0:T(8,128)(2,1)S(1)}, u32[]{:S(2)}, u32[]{:S(2)}) collective-permute-start(bf16[128,512]{1,0:T(8,128)(2,1)S(1)} %get-tuple-element.60), channel_id=1, source_target_pairs={{0,4},{4,8},{8,12},{12,16},{16,20},{20,24},{24,28},{28,32},{32,36}... | collective-permute-start | bytes 393224 | tf_op jit(solution)/shard_map/ppermute | solution.py:285
  69.8 21.9 %all-to-all-start.1 = ((bf16[8,8,1024]{2,1,0:T(8,128)(2,1)}), bf16[8,8,1024]{2,1,0:T(8,128)(2,1)}, u32[]{:S(2)}, u32[]{:S(2)}) async-start(bf16[8,8,1024]{2,1,0:T(8,128)(2,1)} %get-tuple-element.69.rows), calls=%async_computation.1 | async-start | bytes 262144 | tf_op jit(solution)/shard_map/all_to_all | solution.py:286
